TPU v7x, 256 devices: a whole 4x4x8 slice. The times are simulated.
256 devices in a mesh: row: 32 (over y, x, core), col: 8 (over z).
Axes of the slice: x: 4, y: 4, z: 8, core: 2. Of those that a mesh axis runs over, the one named last changes fastest.
Arguments:
- matrix: float32 [4, 8192, 4, 2048], P(None, 'row', None, 'col'), may hold values from -12 to 16, as said below
Outputs:
- factored: float32 [4, 8192, 4, 2048], P(None, 'row', None, 'col')
Inputs may be any that keep to these rules, and one draw needn't show every extreme that they name: `matrix`: the leading block of order 2 * 256 is symmetric and positive definite, with all its eigenvalues 4 or more; every other diagonal entry lies between 12 and 16.
All inputs are finite; a program needn't handle non-finite values.
Results may differ from a plain program's by a relative error of at most 0.0001.
Values sent between devices are 32-bit elements; how exact they have to be, the bound alone decides.
No kernel may reach another device: no remote copies, remote signals or barrier semaphores. Data moves between devices by JAX's collectives and lax.ppermute only.
A program may use at most 128 MiB of HBM per device.

v0:
```python
import jax
import jax.numpy as jnp
from jax import lax
from jax.sharding import PartitionSpec as P


def spread(value, axis, source):
    kept = jnp.where(lax.axis_index(axis) == source, value, 0).astype(value.dtype)
    return lax.psum(kept, axis)


def per_device(matrix):
    rows_count = lax.axis_size("row")
    cols_count = lax.axis_size("col")
    group = rows_count // cols_count
    row_index = lax.axis_index("row")
    col_index = lax.axis_index("col")
    tile_rows = matrix.shape[0]
    tile = matrix.shape[1]
    tile_cols = matrix.shape[2]
    global_rows = jnp.arange(tile_rows, dtype=jnp.int32) * rows_count + row_index
    global_cols = jnp.arange(tile_cols, dtype=jnp.int32) * cols_count + col_index
    eye = jnp.eye(tile, dtype=jnp.float32)
    current = matrix
    for k in range(2):
        column = current[:, :, 0, :]
        corner = spread(column[0], "row", k)
        lower = jnp.linalg.cholesky(corner)
        inverse = lax.linalg.triangular_solve(lower, eye, left_side=True, lower=True)
        solved = jnp.einsum(
            "mab,db->mad",
            column,
            inverse,
            precision=lax.Precision.HIGHEST,
            preferred_element_type=jnp.float32,
        )
        picked = jnp.where(
            (global_rows > k)[:, None, None],
            solved,
            jnp.where((global_rows == k)[:, None, None], lower[None], 0.0),
        )
        factor_row_panel = spread(picked, "col", k)
        share = factor_row_panel[: tile_cols // group]
        every = lax.all_gather(share, "row", axis=0, tiled=True)
        every = every.reshape(group, cols_count, tile_cols // group, tile, tile)
        owned = lax.dynamic_index_in_dim(every, col_index, 1, keepdims=False)
        factor_mirrored = jnp.swapaxes(owned, 0, 1).reshape(tile_cols, tile, tile)
        product = jnp.einsum(
            "mad,nbd->manb",
            factor_row_panel,
            factor_mirrored,
            precision=lax.Precision.HIGHEST,
            preferred_element_type=jnp.float32,
        )
        keep = (global_rows > k)[:, None, None, None] & (global_cols > k)[None, None, :, None]
        fresh = jnp.where(keep, current - product, current)
        place = (global_cols == k)[None, None, :, None]
        current = jnp.where(place, factor_row_panel[:, :, None, :], fresh)
    return current


def solution(mesh):
    in_specs = (P(None, "row", None, "col"),)
    out_specs = P(None, "row", None, "col")
    return jax.shard_map(
        per_device, mesh=mesh, in_specs=in_specs, out_specs=out_specs, check_vma=False
    )
```

profile of v0, /device:TPU:1, one launch (start us, length us, event | category | flops | bytes accessed | tf_op | source)
XLA Modules:
  0.0 673.6 jit_solution(7971984366747209886)
XLA Ops:
  6.5 5.2 copy.19
  11.8 1.7 fusion.12
  13.6 115.2 %all-reduce.6.cloned.1.call-done = f32[256,256]{0,1:T(8,128)} async-done(((f32[256,256]{0,1:T(8,128)}), f32[256,256]{0,1:T(8,128)}) %all-reduce.6.cloned.1.call-update) | async-done | bytes 262160 | tf_op jit(solution)/shard_map/psum | solution.py:9
  130.8 11.7 %cholesky.130 = f32[128,128]{1,0:T(8,128)S(1)} custom-call(f32[128,128]{1,0:T(8,128)S(1)} %cholesky.194), custom_call_target="Cholesky" | custom-call | tf_op jit(solution)/shard_map/jit(cholesky)/cholesky | solution.py:28
  142.6 9.8 %custom-call.13 = f32[1,128,128]{1,2,0:T(8,128)S(1)} custom-call(f32[1,128,128]{2,1,0:T(8,128)S(1)} %get-tuple-element.54), custom_call_target="InvertDiagBlocksLowerTriangular" | custom-call | tf_op jit(solution)/shard_map/jit(cholesky)/cholesky | solution.py:28
  152.9 11.7 %cholesky.147 = f32[128,128]{1,0:T(8,128)S(1)} custom-call(f32[128,128]{1,0:T(8,128)S(1)} %convolution_subtract_fusion.3), custom_call_target="Cholesky" | custom-call | tf_op jit(solution)/shard_map/jit(cholesky)/cholesky | solution.py:28
  166.7 4.5 while.4
  171.2 19.7 %custom-call.14 = f32[2,128,128]{1,2,0:T(8,128)S(1)} custom-call(f32[2,128,128]{2,1,0:T(8,128)S(1)} %get-tuple-element.21), custom_call_target="InvertDiagBlocksLowerTriangular" | custom-call | tf_op jit(solution)/shard_map/triangular_solve/custom-call.0 | solution.py:29
  192.0 2.1 fusion.4
  194.1 71.7 %all-reduce.8.cloned.1.call-done = f32[4,256,256]{1,2,0:T(8,128)} async-done(((f32[4,256,256]{1,2,0:T(8,128)}), f32[4,256,256]{1,2,0:T(8,128)}) %all-reduce.8.cloned.1.call-update) | async-done | bytes 1048592 | tf_op jit(solution)/shard_map/psum | solution.py:9
  267.8 61.9 %all-gather.3.cloned.1.call-done = f32[32,256,256]{2,1,0:T(8,128)} async-done(((f32[1,256,256]{2,1,0:T(8,128)}), f32[32,256,256]{2,1,0:T(8,128)}) %all-gather.3.cloned.1.call-update) | async-done | bytes 8388624 | tf_op jit(solution)/shard_map/all_gather | solution.py:44
  329.7 7.1 %fusion = f32[4,256,4,256]{1,3,2,0:T(8,128)S(1)} fusion(f32[4,256,4,256]{1,3,2,0:T(8,128)} %copy.19, f32[4,256,256]{1,2,0:T(8,128)} %all-reduce.8.cloned.1.call-done, pred[4]{0:T(512)(128)(4,1)S(1)} %get-tuple-element.64, pred[4,4]{1,0:T(4,128)(4,1)S(1)} %broadcast_and_fusion.1, f32[4,8,1,256,256]{4,3,1,0,2:T(8,128)} %bitcast.110, s32[]{:T(128)S(6)} %select_n.78), kind=kOutput, calls=%fused_computation.6 | convolution fusion | flops 3224371200 | bytes 11534360 | tf_op jit(solution)/shard_map/mad,nbd->manb/dot_general | solution.py:48
  336.9 2.0 copy-done
  339.8 110.5 %all-reduce.10.cloned.1.call-done = f32[256,256]{0,1:T(8,128)} async-done(((f32[256,256]{0,1:T(8,128)}), f32[256,256]{0,1:T(8,128)}) %all-reduce.10.cloned.1.call-update) | async-done | bytes 262160 | tf_op jit(solution)/shard_map/psum | solution.py:9
  452.4 11.7 %cholesky.164 = f32[128,128]{1,0:T(8,128)S(1)} custom-call(f32[128,128]{1,0:T(8,128)S(1)} %cholesky.197), custom_call_target="Cholesky" | custom-call | tf_op jit(solution)/shard_map/jit(cholesky)/cholesky | solution.py:28
  464.2 9.8 %custom-call.15 = f32[1,128,128]{1,2,0:T(8,128)S(1)} custom-call(f32[1,128,128]{2,1,0:T(8,128)S(1)} %get-tuple-element.50), custom_call_target="InvertDiagBlocksLowerTriangular" | custom-call | tf_op jit(solution)/shard_map/jit(cholesky)/cholesky | solution.py:28
  474.5 11.7 %cholesky.181 = f32[128,128]{1,0:T(8,128)S(1)} custom-call(f32[128,128]{1,0:T(8,128)S(1)} %convolution_subtract_fusion.2), custom_call_target="Cholesky" | custom-call | tf_op jit(solution)/shard_map/jit(cholesky)/cholesky | solution.py:28
  488.9 4.2 while.5
  493.1 19.7 %custom-call.16 = f32[2,128,128]{1,2,0:T(8,128)S(1)} custom-call(f32[2,128,128]{2,1,0:T(8,128)S(1)} %get-tuple-element.22), custom_call_target="InvertDiagBlocksLowerTriangular" | custom-call | tf_op jit(solution)/shard_map/triangular_solve/custom-call.0 | solution.py:29
  513.9 3.3 fusion.2
  517.3 71.7 %all-reduce.12.cloned.1.call-done = f32[4,256,256]{1,2,0:T(8,128)} async-done(((f32[4,256,256]{1,2,0:T(8,128)}), f32[4,256,256]{1,2,0:T(8,128)}) %all-reduce.12.cloned.1.call-update) | async-done | bytes 1048592 | tf_op jit(solution)/shard_map/psum | solution.py:9
  590.9 61.3 %all-gather.5.cloned.1.call-done = f32[32,256,256]{2,1,0:T(8,128)} async-done(((f32[1,256,256]{2,1,0:T(8,128)}), f32[32,256,256]{2,1,0:T(8,128)}) %all-gather.5.cloned.1.call-update) | async-done | bytes 8388624 | tf_op jit(solution)/shard_map/all_gather | solution.py:44
  652.2 9.1 %fusion.1 = f32[4,256,4,256]{1,3,2,0:T(8,128)} fusion(f32[4,256,4,256]{1,3,2,0:T(8,128)} %copy-done, f32[4,256,256]{1,2,0:T(8,128)} %all-reduce.12.cloned.1.call-done, pred[4]{0:T(512)(128)(4,1)S(1)} %get-tuple-element.68, pred[4,4]{1,0:T(4,128)(4,1)S(1)} %broadcast_and_fusion, f32[4,8,1,256,256]{4,3,1,0,2:T(8,128)} %bitcast.111, s32[]{:T(128)S(6)} %select_n.78), kind=kOutput, calls=%fused_computation.7 | convolution fusion | flops 3224371200 | bytes 11534360 | tf_op jit(solution)/shard_map/mad,nbd->manb/dot_general | solution.py:48
  661.3 5.2 copy.37
  (72 shorter events, 22.5 us)
Async XLA Ops:
  6.5 122.2 %all-reduce.6.cloned.1.call-start = ((), (), s32[]{:S(2)}) async-start(), calls=%async_computation | async-start | bytes 524288 | tf_op jit(solution)/shard_map/psum | solution.py:9
  13.5 178.5 %slice-start = ((f32[4,256,4,256]{3,2,1,0:T(4,128)}), f32[4,256,1,256]{3,2,1,0:T(1,128)S(1)}, s32[]{:S(2)}) async-start(f32[4,256,4,256]{3,2,1,0:T(4,128)} %param.4), calls=%async_computation.6 | async-start | bytes 2097152 | tf_op jit(solution)/shard_map/slice | solution.py:26
  13.5 252.4 %all-reduce.8.cloned.1.call-start = ((), (), s32[]{:S(2)}) async-start(), calls=%async_computation.1 | async-start | bytes 2097152 | tf_op jit(solution)/shard_map/psum | solution.py:9
  194.1 135.6 %all-gather.3.cloned.1.call-start = ((), (), s32[]{:S(2)}) async-start(), calls=%async_computation.2 | async-start | bytes 8650752 | tf_op jit(solution)/shard_map/all_gather | solution.py:44
  267.7 182.6 %all-reduce.10.cloned.1.call-start = ((), (), s32[]{:S(2)}) async-start(), calls=%async_computation.3 | async-start | bytes 524288 | tf_op jit(solution)/shard_map/psum | solution.py:9
  336.8 2.0 copy-start
  339.6 249.4 %all-reduce.12.cloned.1.call-start = ((), (), s32[]{:S(2)}) async-start(), calls=%async_computation.4 | async-start | bytes 2097152 | tf_op jit(solution)/shard_map/psum | solution.py:9
  517.2 135.0 %all-gather.5.cloned.1.call-start = ((), (), s32[]{:S(2)}) async-start(), calls=%async_computation.5 | async-start | bytes 8650752 | tf_op jit(solution)/shard_map/all_gather | solution.py:44
Sparse Core Ops, SparseCore 0:
  13.6 115.1 all-reduce.5
  194.2 71.6 all-reduce.7
  268.8 60.8 all-gather.2
  339.7 110.5 all-reduce.9
  517.3 71.5 all-reduce.11
  591.4 60.7 all-gather.4
where the time goes:
time: 682 us; the launch traced here: 674 us
  waiting for transfers between devices  492 us (72%)
  other arithmetic  113 us (17%)
  local copies, waits for them, and re-layouts  26.6 us (4%)
  matrix products  24.4 us (4%)
  between operations  16.5 us (2%)
    psum x4, waiting for transfers between devices, spread(): return lax.psum(kept, axis)  369 us
    all_gather x2, waiting for transfers between devices, per_device(): every = lax.all_gather(share, 'row', axis=0, tiled=True)  123 us
    another operation x13, other arithmetic, per_device(): lower = jnp.linalg.cholesky(corner)  68.7 us
    another operation x5, other arithmetic, per_device(): lax.linalg.triangular_solve(lower, eye, left_side=True, lower=True)  39.4 us
    dot_general x2, matrix products, per_device(): jnp.einsum('mad,nbd->manb', factor_row_panel, factor_mirrored, precision=...  16.2 us
  transfers between devices with their start and end apart: 6, of which 6 were waited for; matrix products, arithmetic and copies ran while one was open for 0% of the time, Pallas kernels for 0%

commit v1 on v0

v1 whole, which is shorter than its diff:
```python
import jax
import jax.numpy as jnp
from jax import lax
from jax.experimental import pallas as pl
from jax.experimental.pallas import tpu as pltpu
from jax.sharding import PartitionSpec as P

HI = lax.Precision.HIGHEST
F32 = jnp.float32
BF16 = jnp.bfloat16
B = 128
T = 256
MIB = 1024 * 1024


def dot(a, b):
    return lax.dot_general(a, b, (((1,), (0,)), ((), ())), precision=HI, preferred_element_type=F32)


def dot_t(a, b):
    return lax.dot_general(a, b, (((1,), (1,)), ((), ())), precision=HI, preferred_element_type=F32)


def leaf(d):
    n = d.shape[0]
    sub = lax.broadcasted_iota(jnp.int32, (8, B), 0)
    row = lax.broadcasted_iota(jnp.int32, (n, B), 0)
    col = lax.broadcasted_iota(jnp.int32, (n, B), 1)
    e = jnp.where(row == col, 1.0, 0.0).astype(F32)
    out = []
    for q in range(n // 8):
        left = n - 8 * q
        rest = left - 8
        cols = [jnp.broadcast_to(d[:, 8 * q + k : 8 * q + k + 1], (left, B)) for k in range(8)]
        tops, lows = [], []
        scale = jnp.zeros((8, B), F32)
        for k in range(8):
            pivot = jnp.broadcast_to(cols[k][k : k + 1, :], (8, B))
            reciprocal = 1.0 / pivot
            scale = jnp.where(sub == k, lax.rsqrt(pivot), scale)
            top = jnp.where(sub > k, cols[k][:8] * reciprocal, 0.0)
            tops.append(top)
            if rest:
                low = cols[k][8:] * jnp.broadcast_to(reciprocal[:1], (rest, B))
                lows.append(low)
            for l in range(k + 1, 8):
                u = cols[l][k : k + 1, :]
                t = cols[l][:8] - top * jnp.broadcast_to(u, (8, B))
                if rest:
                    r = cols[l][8:] - low * jnp.broadcast_to(u, (rest, B))
                    t = jnp.concatenate([t, r], 0)
                cols[l] = t
        d_top, e_top = d[:8], e[:8]
        d_rows, e_rows = [], []
        for k in range(8):
            a, b = d_top[k : k + 1, :], e_top[k : k + 1, :]
            d_rows.append(a)
            e_rows.append(b)
            d_top = d_top - tops[k] * jnp.broadcast_to(a, (8, B))
            e_top = e_top - tops[k] * jnp.broadcast_to(b, (8, B))
        out.append(e_top * scale)
        if rest:
            d, e = d[8:], e[8:]
            for k in range(8):
                d = d - lows[k] * jnp.broadcast_to(d_rows[k], (rest, B))
                e = e - lows[k] * jnp.broadcast_to(e_rows[k], (rest, B))
    return jnp.concatenate(out, 0)


def factor_kernel(s00, s10, s11, w, a, e):
    a[0:T, 0:T] = 0.5 * (s00[...] + s00[...].T)
    a[T:, 0:T] = s10[...]
    a[T:, T:] = 0.5 * (s11[...] + s11[...].T)
    w[...] = jnp.zeros_like(w)
    e[...] = jnp.zeros_like(e)
    for i in range(4):
        o = i * B
        p = o + B
        part = leaf(a[o:p, o:p])
        w[o:p, o:p] = part
        if i:
            w[o:p, 0:o] = dot(part, e[o:p, 0:o])
        if i < 3:
            low = dot_t(a[p:, o:p], part)
            for j in range(i + 1, 4):
                r = (j - i - 1) * B
                a[j * B :, j * B : (j + 1) * B] -= dot_t(low[r:], low[r : r + B])
            e[p:, 0:p] -= dot(low, w[o:p, 0:p])


def factor(s00, s10, s11):
    vmem = pl.BlockSpec(memory_space=pltpu.VMEM)
    return pl.pallas_call(
        factor_kernel,
        out_shape=jax.ShapeDtypeStruct((2 * T, 2 * T), F32),
        in_specs=[vmem] * 3,
        out_specs=vmem,
        scratch_shapes=[pltpu.VMEM((2 * T, 2 * T), F32)] * 2,
        compiler_params=pltpu.CompilerParams(vmem_limit_bytes=16 * MIB),
        cost_estimate=pl.CostEstimate(flops=10**9, bytes_accessed=2 * MIB, transcendentals=0),
    )(s00, s10, s11)


def split(x):
    high = x.astype(BF16)
    return high, (x - high.astype(F32)).astype(BF16)


def update_kernel(where, a, p, g0, g1, g2, g3, h0, h1, h2, h3, w, out, mirror, y_high, y_low):
    r, c = where[0], where[1]
    m = pl.program_id(0)
    core = lax.rem(r, 2)
    y = r // 8

    def solve(first, second):
        x0 = dot_t(first, w[0:T, 0:T])
        x1 = dot_t(first, w[T:, 0:T]) + dot_t(second, w[T:, T:])
        return x0, x1

    @pl.when(m == 0)
    def _():
        for s, (g, h) in enumerate(((g0, h0), (g1, h1), (g2, h2), (g3, h3))):
            n = lax.rem(y - s + 4, 4)
            mirror[core, n] = g[...]
            mirror[1 - core, n] = h[...]
        for n in range(4):
            x0, x1 = solve(mirror[0, n], mirror[1, n])
            tile = n * 8 + c
            x0 = jnp.where(tile > 0, x0, 0.0)
            x1 = jnp.where(tile > 1, x1, 0.0)
            for k, x in enumerate((x0, x1)):
                high, low = split(x)
                y_high[n * T : (n + 1) * T, k * T : (k + 1) * T] = high
                y_low[n * T : (n + 1) * T, k * T : (k + 1) * T] = low

    x0, x1 = solve(p[:, 0].reshape(T, T), p[:, 1].reshape(T, T))
    tile = m * 32 + r
    u0 = jnp.where(tile > 0, x0, 0.0)
    u1 = jnp.where(tile > 1, x1, 0.0)
    x_high, x_low = split(jnp.concatenate([u0, u1], axis=1))

    def mul(u, v):
        return lax.dot_general(u, v, (((1,), (1,)), ((), ())), preferred_element_type=F32)

    for n in range(4):
        span = slice(n * T, (n + 1) * T)
        product = mul(x_high, y_high[span]) + mul(x_high, y_low[span]) + mul(x_low, y_high[span])
        for half in range(2):
            at = pl.ds(half * 4 + n, T, stride=8)
            out[at, :] = a[at, :] - product[:, half * B : (half + 1) * B]

    @pl.when(c < 2)
    def _():
        row = lax.broadcasted_iota(jnp.int32, (T, T), 0)
        col = lax.broadcasted_iota(jnp.int32, (T, T), 1)
        x = jnp.where(c == 0, x0, x1)
        keep = (tile > c) | ((tile == c) & (row >= col))
        x = jnp.where(keep, x, 0.0)
        for half in range(2):
            out[pl.ds(half * 4, T, stride=8), :] = x[:, half * B : (half + 1) * B]


def update(where, a, p, g, h, w):
    whole = pl.BlockSpec((T, T), lambda m: (0, 0))
    return pl.pallas_call(
        update_kernel,
        grid=(4,),
        out_shape=jax.ShapeDtypeStruct(a.shape, F32),
        in_specs=[
            pl.BlockSpec(memory_space=pltpu.SMEM),
            pl.BlockSpec((8 * T, B), lambda m: (m, 0)),
            pl.BlockSpec((2, 2, B, T), lambda m: (m, 0, 0, 0)),
        ]
        + [whole] * 8
        + [pl.BlockSpec((2 * T, 2 * T), lambda m: (0, 0))],
        out_specs=pl.BlockSpec((8 * T, B), lambda m: (m, 0)),
        scratch_shapes=[
            pltpu.VMEM((2, 4, T, T), F32),
            pltpu.VMEM((4 * T, 2 * T), BF16),
            pltpu.VMEM((4 * T, 2 * T), BF16),
        ],
        compiler_params=pltpu.CompilerParams(vmem_limit_bytes=32 * MIB),
        cost_estimate=pl.CostEstimate(flops=8 * 10**9, bytes_accessed=12 * MIB, transcendentals=0),
    )(where, a, p, *g, *h, w)


def device(r, c):
    return r * 8 + c


def send(x, pairs):
    return lax.ppermute(x, ("row", "col"), [(device(*a), device(*b)) for a, b in pairs])


def total(x, parts):
    for part in parts:
        x = x + part
    return x


def broadcast(x):
    x = total(x, [send(x, [((0, 0), (8 * s, 0))]) for s in (1, 2, 3)])
    x = total(x, [send(x, [((8 * y, 0), (8 * y + 2 * s, 0)) for y in range(4)]) for s in (1, 2, 3)])
    chips = range(0, 32, 2)
    x = total(x, [send(x, [((r, 0), (r, 2 * s)) for r in chips]) for s in (1, 2, 3)])
    x = total(x, [send(x, [((r, z), (r, z + 1)) for r in chips for z in range(0, 8, 2)])])
    return total(x, [send(x, [((r, z), (r + 1, z)) for r in chips for z in range(8)])])


def per_device(matrix):
    r = lax.axis_index("row")
    c = lax.axis_index("col")
    flat = matrix.reshape(4, T, 4, 2, B).transpose(0, 1, 3, 2, 4).reshape(4 * T * 8, B)
    column = matrix[:, :, 0, :]

    first = column[0]
    origin = (r == 0) & (c == 0)
    s00 = broadcast(jnp.where(origin, first, 0.0))
    s10 = send(first, [((1, 0), (0, 0))])
    s11 = send(first, [((1, 1), (0, 0))])
    rest = broadcast(jnp.concatenate([s10, s11], axis=0))

    chunks = column.reshape(8, B, T)
    got = [lax.dynamic_index_in_dim(chunks, c, 0, keepdims=False)]
    for s in range(1, 8):
        piece = lax.dynamic_index_in_dim(chunks, lax.rem(c + s, 8), 0, keepdims=False)
        got.append(lax.ppermute(piece, "col", [(0, s), (1, (1 + s) % 8)]))
    got = jnp.stack(got)
    mine = [lax.dynamic_index_in_dim(got, lax.rem(c + 8 - k, 8), 0, keepdims=False) for k in range(2)]
    panel = lax.all_gather(jnp.stack(mine), "col", axis=0)

    v = send(first, [((i, k), (i // 2 * 2 + k, i % 8)) for i in range(32) for k in range(2)])
    lanes = [(y, z, k) for y in range(4) for z in range(8) for k in range(2)]
    v = total(
        v,
        [
            send(v, [((8 * y + z // 2 * 2 + k, z), (8 * y + (z // 2 + s) % 4 * 2 + k, z)) for y, z, k in lanes])
            for s in (1, 2, 3)
        ],
    )
    g = [v] + [lax.ppermute(v, "row", [(i, (i + 8 * s) % 32) for i in range(32)]) for s in (1, 2, 3)]
    h = [lax.ppermute(t, "row", [(i, i ^ 1) for i in range(32)]) for t in g]

    w = factor(s00, rest[:T], rest[T:])
    where = jnp.stack([r, c]).astype(jnp.int32)
    out = update(where, flat, panel, g, h, w)
    return out.reshape(4, T, 2, 4, B).transpose(0, 1, 3, 2, 4).reshape(4, T, 4, T)


def solution(mesh):
    spec = P(None, "row", None, "col")
    return jax.shard_map(per_device, mesh=mesh, in_specs=(spec,), out_specs=spec, check_vma=False)
```

time: 682 us -> 183 us (0.27); the launches traced: 674 us -> 182 us
  waiting for transfers between devices: 492 us -> 15.6 us
  other arithmetic: 113 us -> 1.75 us
  starting transfers between devices: 0.38 us -> 105 us
  Pallas kernels: 0 us -> 34.6 us
  matrix products: 24.4 us -> 0 us
  local copies, waits for them, and re-layouts: 26.6 us -> 11 us
    psum x4 -> x0, waiting for transfers between devices: 369 us -> none  [spread(): return lax.psum(kept, axis)]
    all_gather x2 -> x1, waiting for transfers between devices: 123 us -> 0.02 us  [per_device(): panel = lax.all_gather(jnp.stack(mine), 'col', axis=0)]
    another operation x18 -> x2, other arithmetic: 108 us -> 0.8 us  [the longest x1 0.72 us: per_device(): panel = lax.all_gather(jnp.stack(mine), 'col', axis=0)]
    ppermute x0 -> x42, starting transfers between devices: none -> 105 us  [the longest x28 40.9 us: send(): lax.ppermute(x, ('row', 'col'), [(device(*a), device(*b)) for a, b in pai...]
    pallas_call x0 -> x2, Pallas kernels: none -> 34.6 us  [the longest x1 19.5 us: factor(): pl.pallas_call(factor_kernel, out_shape=jax.ShapeDtypeStruct((2 * T, 2 *...]
    dot_general x4 -> x0, matrix products: 21.7 us -> none  [the longest x2 16.2 us: per_device(): jnp.einsum('mad,nbd->manb', factor_row_panel, factor_mirrored, precision=...]
    ppermute x0 -> x42, waiting for transfers between devices: none -> 15.6 us  [the longest x7 8.34 us: per_device(): got.append(lax.ppermute(piece, 'col', [(0, s), (1, (1 + s) % 8)]))]
    another operation x19 -> x1, local copies, waits for them, and re-layouts: 8.08 us -> 0.67 us  [per_device(): got = jnp.stack(got)]
  transfers between devices with their start and end apart: 6 -> 43, of which waited for: 6 -> 7; matrix products, arithmetic and copies ran while one was open for 0% -> 3% of each run, Pallas kernels for 0% -> 11%
where the time goes in v1:
time: 183 us; the launch traced here: 182 us
  starting transfers between devices  105 us (57%)
  Pallas kernels  34.6 us (19%)
  waiting for transfers between devices  15.6 us (9%)
  between operations  14.2 us (8%)
  local copies, waits for them, and re-layouts  11 us (6%)
    ppermute x28, starting transfers between devices, send(): lax.ppermute(x, ('row', 'col'), [(device(*a), device(*b)) for a, b in pai...  40.9 us
    ppermute x4, starting transfers between devices, per_device(): h = [lax.ppermute(t, 'row', [(i, i ^ 1) for i in range(32)]) for t in g]  34.9 us
    ppermute x7, starting transfers between devices, per_device(): got.append(lax.ppermute(piece, 'col', [(0, s), (1, (1 + s) % 8)]))  24.2 us
    pallas_call x1, Pallas kernels, factor(): pl.pallas_call(factor_kernel, out_shape=jax.ShapeDtypeStruct((2 * T, 2 *...  19.5 us
    pallas_call x1, Pallas kernels, update(): pl.pallas_call(update_kernel, grid=(4,), out_shape=jax.ShapeDtypeStruct(a...  15.1 us
    ppermute x7, waiting for transfers between devices, per_device(): got.append(lax.ppermute(piece, 'col', [(0, s), (1, (1 + s) % 8)]))  8.34 us
    ppermute x3, starting transfers between devices, per_device(): lax.ppermute(v, 'row', [(i, (i + 8 * s) % 32) for i in range(32)])  4.99 us
    unnamed x15, local copies, waits for them, and re-layouts  4.91 us
  transfers between devices with their start and end apart: 43, of which 7 were waited for; matrix products, arithmetic and copies ran while one was open for 3% of the time, Pallas kernels for 11%

profile of v1, /device:TPU:1, one launch (start us, length us, event | category | flops | bytes accessed | tf_op | source)
XLA Modules:
  0.0 182.1 jit_solution(9952488500292393918)
XLA Ops:
  6.5 2.9 %slice.14 = f32[4,256,1,256]{3,2,1,0:T(1,128)S(1)} slice(f32[4,256,4,256]{3,2,1,0:T(4,128)} %param.1), slice={[0:4], [0:256], [0:1], [0:256]} | slice | bytes 2097152 | tf_op jit(solution)/shard_map/slice | solution.py:214
  9.7 4.4 %collective-permute-start = (f32[128,256]{1,0:T(8,128)S(1)}, f32[128,256]{1,0:T(8,128)S(1)}, u32[]{:S(2)}, u32[]{:S(2)}) collective-permute-start(f32[128,256]{1,0:T(8,128)S(1)} %get-tuple-element.13), channel_id=1, source_target_pairs={{0,1},{1,2},{8,9},{9,10},{16,17},{17,18},{24,25},{25,26},{32,33},{... | collective-permute-start | bytes 393224 | tf_op jit(solution)/shard_map/ppermute | solution.py:227
  15.5 2.9 %collective-permute-start.29 = (f32[256,256]{1,0:T(8,128)S(1)}, f32[256,256]{1,0:T(8,128)S(1)}, u32[]{:S(2)}, u32[]{:S(2)}) collective-permute-start(f32[256,256]{1,0:T(8,128)S(1)} %bitcast.52), channel_id=1, source_target_pairs={{8,0}} | collective-permute-start | bytes 786440 | tf_op jit(solution)/shard_map/ppermute | solution.py:192
  19.1 2.4 %collective-permute-start.6 = (f32[128,256]{1,0:T(8,128)S(1)}, f32[128,256]{1,0:T(8,128)S(1)}, u32[]{:S(2)}, u32[]{:S(2)}) collective-permute-start(f32[128,256]{1,0:T(8,128)S(1)} %get-tuple-element.7), channel_id=1, source_target_pairs={{0,7},{1,0},{8,15},{9,8},{16,23},{17,16},{24,31},{25,24},{32,39},{... | collective-permute-start | bytes 393224 | tf_op jit(solution)/shard_map/ppermute | solution.py:227
  24.1 2.2 %collective-permute-done.1 = f32[128,256]{1,0:T(8,128)S(1)} collective-permute-done((f32[128,256]{1,0:T(8,128)S(1)}, f32[128,256]{1,0:T(8,128)S(1)}, u32[]{:S(2)}, u32[]{:S(2)}) %collective-permute-start.1) | collective-permute-done | bytes 131104 | tf_op jit(solution)/shard_map/ppermute | solution.py:227
  26.3 9.7 %collective-permute-start.2 = (f32[128,256]{1,0:T(8,128)S(1)}, f32[128,256]{1,0:T(8,128)S(1)}, u32[]{:S(2)}, u32[]{:S(2)}) collective-permute-start(f32[128,256]{1,0:T(8,128)S(1)} %get-tuple-element.11), channel_id=1, source_target_pairs={{0,3},{1,4},{8,11},{9,12},{16,19},{17,20},{24,27},{25,28},{32,35},... | collective-permute-start | bytes 393224 | tf_op jit(solution)/shard_map/ppermute | solution.py:227
  36.0 2.3 %collective-permute-done.2 = f32[128,256]{1,0:T(8,128)S(1)} collective-permute-done((f32[128,256]{1,0:T(8,128)S(1)}, f32[128,256]{1,0:T(8,128)S(1)}, u32[]{:S(2)}, u32[]{:S(2)}) %collective-permute-start.2) | collective-permute-done | bytes 131104 | tf_op jit(solution)/shard_map/ppermute | solution.py:227
  38.3 3.7 %collective-permute-start.3 = (f32[128,256]{1,0:T(8,128)S(1)}, f32[128,256]{1,0:T(8,128)S(1)}, u32[]{:S(2)}, u32[]{:S(2)}) collective-permute-start(f32[128,256]{1,0:T(8,128)S(1)} %get-tuple-element.10), channel_id=1, source_target_pairs={{0,4},{1,5},{8,12},{9,13},{16,20},{17,21},{24,28},{25,29},{32,36},... | collective-permute-start | bytes 393224 | tf_op jit(solution)/shard_map/ppermute | solution.py:227
  42.1 1.9 %collective-permute-done.3 = f32[128,256]{1,0:T(8,128)S(1)} collective-permute-done((f32[128,256]{1,0:T(8,128)S(1)}, f32[128,256]{1,0:T(8,128)S(1)}, u32[]{:S(2)}, u32[]{:S(2)}) %collective-permute-start.3) | collective-permute-done | bytes 131104 | tf_op jit(solution)/shard_map/ppermute | solution.py:227
  44.0 1.4 collective-permute-start.4
  45.4 1.9 %collective-permute-done.4 = f32[128,256]{1,0:T(8,128)S(1)} collective-permute-done((f32[128,256]{1,0:T(8,128)S(1)}, f32[128,256]{1,0:T(8,128)S(1)}, u32[]{:S(2)}, u32[]{:S(2)}) %collective-permute-start.4) | collective-permute-done | bytes 131104 | tf_op jit(solution)/shard_map/ppermute | solution.py:227
  59.6 1.9 %collective-permute-start.7 = (f32[256,256]{1,0:T(8,128)S(1)}, f32[256,256]{1,0:T(8,128)S(1)}, u32[]{:S(2)}, u32[]{:S(2)}) collective-permute-start(f32[256,256]{1,0:T(8,128)S(1)} %bitcast.54), channel_id=1, source_target_pairs={{0,0},{1,8},{8,1},{9,9},{16,18},{17,26},{24,19},{25,27},{32,36},{3... | collective-permute-start | bytes 786440 | tf_op jit(solution)/shard_map/ppermute | solution.py:192
  67.3 4.1 %collective-permute-start.10 = (f32[256,256]{1,0:T(8,128)S(1)}, f32[256,256]{1,0:T(8,128)S(1)}, u32[]{:S(2)}, u32[]{:S(2)}) collective-permute-start(f32[256,256]{1,0:T(8,128)S(1)} %collective-permute-done.7), channel_id=1, source_target_pairs={{0,48},{8,56},{1,49},{9,57},{18,2},{26,10},{19,3},{27,11},{36,20},... | collective-permute-start | bytes 786440 | tf_op jit(solution)/shard_map/ppermute | solution.py:192
  71.4 13.7 %collective-permute-start.9 = (f32[256,256]{1,0:T(8,128)S(1)}, f32[256,256]{1,0:T(8,128)S(1)}, u32[]{:S(2)}, u32[]{:S(2)}) collective-permute-start(f32[256,256]{1,0:T(8,128)S(1)} %collective-permute-done.7), channel_id=1, source_target_pairs={{0,32},{8,40},{1,33},{9,41},{18,50},{26,58},{19,51},{27,59},{36,4}... | collective-permute-start | bytes 786440 | tf_op jit(solution)/shard_map/ppermute | solution.py:192
  88.6 2.6 %collective-permute-done.8 = f32[256,256]{1,0:T(8,128)S(1)} collective-permute-done((f32[256,256]{1,0:T(8,128)S(1)}, f32[256,256]{1,0:T(8,128)S(1)}, u32[]{:S(2)}, u32[]{:S(2)}) %collective-permute-start.8) | collective-permute-done | bytes 262176 | tf_op jit(solution)/shard_map/ppermute | solution.py:192
  91.3 4.3 %collective-permute-start.13 = (f32[256,256]{1,0:T(8,128)S(1)}, f32[256,256]{1,0:T(8,128)S(1)}, u32[]{:S(2)}, u32[]{:S(2)}) collective-permute-start(f32[256,256]{1,0:T(8,128)S(1)} %add_add_fusion.6.g0), channel_id=1, source_target_pairs={{0,192},{8,200},{16,208},{24,216},{32,224},{40,232},{48,240},{56,2... | collective-permute-start | bytes 786440 | tf_op jit(solution)/shard_map/ppermute | solution.py:241
  97.7 4.0 %collective-permute-done.13.g3 = f32[256,256]{1,0:T(8,128)S(1)} collective-permute-done((f32[256,256]{1,0:T(8,128)S(1)}, f32[256,256]{1,0:T(8,128)S(1)}, u32[]{:S(2)}, u32[]{:S(2)}) %collective-permute-start.13) | collective-permute-done | bytes 262176 | tf_op jit(solution)/shard_map/ppermute | solution.py:241
  101.7 30.0 %collective-permute-start.14 = (f32[256,256]{1,0:T(8,128)S(1)}, f32[256,256]{1,0:T(8,128)S(1)}, u32[]{:S(2)}, u32[]{:S(2)}) collective-permute-start(f32[256,256]{1,0:T(8,128)S(1)} %add_add_fusion.6.g0), channel_id=1, source_target_pairs={{0,8},{8,0},{16,24},{24,16},{32,40},{40,32},{48,56},{56,48},{64,72... | collective-permute-start | bytes 786440 | tf_op jit(solution)/shard_map/ppermute | solution.py:242
  131.7 1.8 collective-permute-start.17
  133.6 3.1 %collective-permute-start.16 = (f32[256,256]{1,0:T(8,128)S(1)}, f32[256,256]{1,0:T(8,128)S(1)}, u32[]{:S(2)}, u32[]{:S(2)}) collective-permute-start(f32[256,256]{1,0:T(8,128)S(1)} %collective-permute-done.12.g2), channel_id=1, source_target_pairs={{0,8},{8,0},{16,24},{24,16},{32,40},{40,32},{48,56},{56,48},{64,72... | collective-permute-start | bytes 786440 | tf_op jit(solution)/shard_map/ppermute | solution.py:242
  136.8 19.5 %shard_map.17.w = f32[512,512]{1,0:T(8,128)S(1)} custom-call(f32[256,256]{1,0:T(8,128)S(1)} %add.159.s00, f32[256,256]{1,0:T(8,128)S(1)} %get-tuple-element.16.s10, f32[256,256]{1,0:T(8,128)S(1)} %get-tuple-element.15.s11), custom_call_target="tpu_custom_call" | custom-call | flops 1000000000 | bytes 2097152 | tf_op jit(solution)/shard_map/pallas_call | solution.py:93
  156.4 2.2 %copy-done = f32[4,256,4,256]{3,2,1,0:T(4,128)S(1)} copy-done((f32[4,256,4,256]{3,2,1,0:T(4,128)S(1)}, f32[4,256,4,256]{3,2,1,0:T(4,128)}, u32[]{:S(2)}) %copy-start) | copy-done | bytes 4194328
  158.6 1.6 copy-done.1
  160.2 15.1 %shard_map.18 = f32[8192,128]{1,0:T(8,128)} custom-call(s32[2]{0:T(128)S(1)} %pad_add_fusion.where, f32[8192,128]{1,0:T(8,128)S(1)} %bitcast.49, f32[8,2,128,256]{3,2,1,0:T(8,128)S(1)} %bitcast.50, f32[256,256]{1,0:T(8,128)S(1)} %add_add_fusion.6.g0, f32[256,256]{1,0:T(8,128)S(1)} %collective-permute-done.11.g1, f32[256,256]{1,0:T(8,128)S(1)} %collective-permute-done.12.g2, ...), custom_call_target="tpu_custom_call" | custom-call | flops 8000000000 | bytes 12582912 | tf_op jit(solution)/shard_map/pallas_call | solution.py:165
  (101 shorter events, 28.4 us)
Async XLA Ops:
  6.5 149.9 %all-gather.3.cloned.1.call-start = ((), (), s32[]{:S(2)}) async-start(), calls=%async_computation | async-start | bytes 2359296 | tf_op jit(solution)/shard_map/all_gather | solution.py:230
  9.7 13.1 %collective-permute-start = (f32[128,256]{1,0:T(8,128)S(1)}, f32[128,256]{1,0:T(8,128)S(1)}, u32[]{:S(2)}, u32[]{:S(2)}) collective-permute-start(f32[128,256]{1,0:T(8,128)S(1)} %get-tuple-element.13), channel_id=1, source_target_pairs={{0,1},{1,2},{8,9},{9,10},{16,17},{17,18},{24,25},{25,26},{32,33},{... | collective-permute-start | bytes 393224 | tf_op jit(solution)/shard_map/ppermute | solution.py:227
  15.5 32.9 %collective-permute-start.29 = (f32[256,256]{1,0:T(8,128)S(1)}, f32[256,256]{1,0:T(8,128)S(1)}, u32[]{:S(2)}, u32[]{:S(2)}) collective-permute-start(f32[256,256]{1,0:T(8,128)S(1)} %bitcast.52), channel_id=1, source_target_pairs={{8,0}} | collective-permute-start | bytes 786440 | tf_op jit(solution)/shard_map/ppermute | solution.py:192
  18.4 30.0 %collective-permute-start.30 = (f32[256,256]{1,0:T(8,128)S(1)}, f32[256,256]{1,0:T(8,128)S(1)}, u32[]{:S(2)}, u32[]{:S(2)}) collective-permute-start(f32[256,256]{1,0:T(8,128)S(1)} %bitcast.53), channel_id=1, source_target_pairs={{9,0}} | collective-permute-start | bytes 786440 | tf_op jit(solution)/shard_map/ppermute | solution.py:192
  19.1 31.5 %collective-permute-start.6 = (f32[128,256]{1,0:T(8,128)S(1)}, f32[128,256]{1,0:T(8,128)S(1)}, u32[]{:S(2)}, u32[]{:S(2)}) collective-permute-start(f32[128,256]{1,0:T(8,128)S(1)} %get-tuple-element.7), channel_id=1, source_target_pairs={{0,7},{1,0},{8,15},{9,8},{16,23},{17,16},{24,31},{25,24},{32,39},{... | collective-permute-start | bytes 393224 | tf_op jit(solution)/shard_map/ppermute | solution.py:227
  21.5 25.9 %collective-permute-start.5 = (f32[128,256]{1,0:T(8,128)S(1)}, f32[128,256]{1,0:T(8,128)S(1)}, u32[]{:S(2)}, u32[]{:S(2)}) collective-permute-start(f32[128,256]{1,0:T(8,128)S(1)} %get-tuple-element.8), channel_id=1, source_target_pairs={{0,6},{1,7},{8,14},{9,15},{16,22},{17,23},{24,30},{25,31},{32,38},... | collective-permute-start | bytes 393224 | tf_op jit(solution)/shard_map/ppermute | solution.py:227
  26.3 12.0 %collective-permute-start.2 = (f32[128,256]{1,0:T(8,128)S(1)}, f32[128,256]{1,0:T(8,128)S(1)}, u32[]{:S(2)}, u32[]{:S(2)}) collective-permute-start(f32[128,256]{1,0:T(8,128)S(1)} %get-tuple-element.11), channel_id=1, source_target_pairs={{0,3},{1,4},{8,11},{9,12},{16,19},{17,20},{24,27},{25,28},{32,35},... | collective-permute-start | bytes 393224 | tf_op jit(solution)/shard_map/ppermute | solution.py:227
  59.6 7.7 %collective-permute-start.7 = (f32[256,256]{1,0:T(8,128)S(1)}, f32[256,256]{1,0:T(8,128)S(1)}, u32[]{:S(2)}, u32[]{:S(2)}) collective-permute-start(f32[256,256]{1,0:T(8,128)S(1)} %bitcast.54), channel_id=1, source_target_pairs={{0,0},{1,8},{8,1},{9,9},{16,18},{17,26},{24,19},{25,27},{32,36},{3... | collective-permute-start | bytes 786440 | tf_op jit(solution)/shard_map/ppermute | solution.py:192
  63.9 23.3 %collective-permute-start.40 = (f32[512,256]{1,0:T(8,128)S(1)}, f32[512,256]{1,0:T(8,128)S(1)}, u32[]{:S(2)}, u32[]{:S(2)}) collective-permute-start(f32[512,256]{1,0:T(8,128)S(1)} %add_add_fusion), channel_id=1, source_target_pairs={{0,1},{2,3},{4,5},{6,7},{16,17},{18,19},{20,21},{22,23},{32,33},{3... | collective-permute-start | bytes 1572872 | tf_op jit(solution)/shard_map/ppermute | solution.py:192
  64.7 6.7 %collective-permute-start.26 = (f32[256,256]{1,0:T(8,128)S(1)}, f32[256,256]{1,0:T(8,128)S(1)}, u32[]{:S(2)}, u32[]{:S(2)}) collective-permute-start(f32[256,256]{1,0:T(8,128)S(1)} %add_add_fusion.4), channel_id=1, source_target_pairs={{0,6},{16,22},{32,38},{48,54},{64,70},{80,86},{96,102},{112,118},{... | collective-permute-start | bytes 786440 | tf_op jit(solution)/shard_map/ppermute | solution.py:192
  65.4 19.7 %collective-permute-start.25 = (f32[256,256]{1,0:T(8,128)S(1)}, f32[256,256]{1,0:T(8,128)S(1)}, u32[]{:S(2)}, u32[]{:S(2)}) collective-permute-start(f32[256,256]{1,0:T(8,128)S(1)} %add_add_fusion.4), channel_id=1, source_target_pairs={{0,4},{16,20},{32,36},{48,52},{64,68},{80,84},{96,100},{112,116},{... | collective-permute-start | bytes 786440 | tf_op jit(solution)/shard_map/ppermute | solution.py:192
  66.1 20.4 %collective-permute-start.24 = (f32[256,256]{1,0:T(8,128)S(1)}, f32[256,256]{1,0:T(8,128)S(1)}, u32[]{:S(2)}, u32[]{:S(2)}) collective-permute-start(f32[256,256]{1,0:T(8,128)S(1)} %add_add_fusion.4), channel_id=1, source_target_pairs={{0,2},{16,18},{32,34},{48,50},{64,66},{80,82},{96,98},{112,114},{1... | collective-permute-start | bytes 786440 | tf_op jit(solution)/shard_map/ppermute | solution.py:192
  67.3 21.3 %collective-permute-start.10 = (f32[256,256]{1,0:T(8,128)S(1)}, f32[256,256]{1,0:T(8,128)S(1)}, u32[]{:S(2)}, u32[]{:S(2)}) collective-permute-start(f32[256,256]{1,0:T(8,128)S(1)} %collective-permute-done.7), channel_id=1, source_target_pairs={{0,48},{8,56},{1,49},{9,57},{18,2},{26,10},{19,3},{27,11},{36,20},... | collective-permute-start | bytes 786440 | tf_op jit(solution)/shard_map/ppermute | solution.py:192
  71.4 17.2 %collective-permute-start.9 = (f32[256,256]{1,0:T(8,128)S(1)}, f32[256,256]{1,0:T(8,128)S(1)}, u32[]{:S(2)}, u32[]{:S(2)}) collective-permute-start(f32[256,256]{1,0:T(8,128)S(1)} %collective-permute-done.7), channel_id=1, source_target_pairs={{0,32},{8,40},{1,33},{9,41},{18,50},{26,58},{19,51},{27,59},{36,4}... | collective-permute-start | bytes 786440 | tf_op jit(solution)/shard_map/ppermute | solution.py:192
  86.5 9.8 %collective-permute-start.27 = (f32[256,256]{1,0:T(8,128)S(1)}, f32[256,256]{1,0:T(8,128)S(1)}, u32[]{:S(2)}, u32[]{:S(2)}) collective-permute-start(f32[256,256]{1,0:T(8,128)S(1)} %add_add_fusion.3), channel_id=1, source_target_pairs={{0,1},{2,3},{4,5},{6,7},{16,17},{18,19},{20,21},{22,23},{32,33},{3... | collective-permute-start | bytes 786440 | tf_op jit(solution)/shard_map/ppermute | solution.py:192
  87.3 49.4 %collective-permute-start.41 = (f32[512,256]{1,0:T(8,128)S(1)}, f32[512,256]{1,0:T(8,128)S(1)}, u32[]{:S(2)}, u32[]{:S(2)}) collective-permute-start(f32[512,256]{1,0:T(8,128)S(1)} %add.169), channel_id=1, source_target_pairs={{0,8},{1,9},{2,10},{3,11},{4,12},{5,13},{6,14},{7,15},{16,24},{17,... | collective-permute-start | bytes 1572872 | tf_op jit(solution)/shard_map/ppermute | solution.py:192
  91.3 10.4 %collective-permute-start.13 = (f32[256,256]{1,0:T(8,128)S(1)}, f32[256,256]{1,0:T(8,128)S(1)}, u32[]{:S(2)}, u32[]{:S(2)}) collective-permute-start(f32[256,256]{1,0:T(8,128)S(1)} %add_add_fusion.6.g0), channel_id=1, source_target_pairs={{0,192},{8,200},{16,208},{24,216},{32,224},{40,232},{48,240},{56,2... | collective-permute-start | bytes 786440 | tf_op jit(solution)/shard_map/ppermute | solution.py:241
  95.6 36.1 %collective-permute-start.12 = (f32[256,256]{1,0:T(8,128)S(1)}, f32[256,256]{1,0:T(8,128)S(1)}, u32[]{:S(2)}, u32[]{:S(2)}) collective-permute-start(f32[256,256]{1,0:T(8,128)S(1)} %add_add_fusion.6.g0), channel_id=1, source_target_pairs={{0,128},{8,136},{16,144},{24,152},{32,160},{40,168},{48,176},{56,1... | collective-permute-start | bytes 786440 | tf_op jit(solution)/shard_map/ppermute | solution.py:241
  95.6 37.9 %collective-permute-start.11 = (f32[256,256]{1,0:T(8,128)S(1)}, f32[256,256]{1,0:T(8,128)S(1)}, u32[]{:S(2)}, u32[]{:S(2)}) collective-permute-start(f32[256,256]{1,0:T(8,128)S(1)} %add_add_fusion.6.g0), channel_id=1, source_target_pairs={{0,64},{8,72},{16,80},{24,88},{32,96},{40,104},{48,112},{56,120},{... | collective-permute-start | bytes 786440 | tf_op jit(solution)/shard_map/ppermute | solution.py:241
  96.3 40.3 %collective-permute-start.28 = (f32[256,256]{1,0:T(8,128)S(1)}, f32[256,256]{1,0:T(8,128)S(1)}, u32[]{:S(2)}, u32[]{:S(2)}) collective-permute-start(f32[256,256]{1,0:T(8,128)S(1)} %add.158), channel_id=1, source_target_pairs={{0,8},{1,9},{2,10},{3,11},{4,12},{5,13},{6,14},{7,15},{16,24},{17,... | collective-permute-start | bytes 786440 | tf_op jit(solution)/shard_map/ppermute | solution.py:192
  101.7 54.6 %collective-permute-start.14 = (f32[256,256]{1,0:T(8,128)S(1)}, f32[256,256]{1,0:T(8,128)S(1)}, u32[]{:S(2)}, u32[]{:S(2)}) collective-permute-start(f32[256,256]{1,0:T(8,128)S(1)} %add_add_fusion.6.g0), channel_id=1, source_target_pairs={{0,8},{8,0},{16,24},{24,16},{32,40},{40,32},{48,56},{56,48},{64,72... | collective-permute-start | bytes 786440 | tf_op jit(solution)/shard_map/ppermute | solution.py:242
  131.7 24.6 %collective-permute-start.17 = (f32[256,256]{1,0:T(8,128)S(1)}, f32[256,256]{1,0:T(8,128)S(1)}, u32[]{:S(2)}, u32[]{:S(2)}) collective-permute-start(f32[256,256]{1,0:T(8,128)S(1)} %collective-permute-done.13.g3), channel_id=1, source_target_pairs={{0,8},{8,0},{16,24},{24,16},{32,40},{40,32},{48,56},{56,48},{64,72... | collective-permute-start | bytes 786440 | tf_op jit(solution)/shard_map/ppermute | solution.py:242
  133.6 22.8 %collective-permute-start.16 = (f32[256,256]{1,0:T(8,128)S(1)}, f32[256,256]{1,0:T(8,128)S(1)}, u32[]{:S(2)}, u32[]{:S(2)}) collective-permute-start(f32[256,256]{1,0:T(8,128)S(1)} %collective-permute-done.12.g2), channel_id=1, source_target_pairs={{0,8},{8,0},{16,24},{24,16},{32,40},{40,32},{48,56},{56,48},{64,72... | collective-permute-start | bytes 786440 | tf_op jit(solution)/shard_map/ppermute | solution.py:242
  136.7 19.7 %collective-permute-start.15 = (f32[256,256]{1,0:T(8,128)S(1)}, f32[256,256]{1,0:T(8,128)S(1)}, u32[]{:S(2)}, u32[]{:S(2)}) collective-permute-start(f32[256,256]{1,0:T(8,128)S(1)} %collective-permute-done.11.g1), channel_id=1, source_target_pairs={{0,8},{8,0},{16,24},{24,16},{32,40},{40,32},{48,56},{56,48},{64,72... | collective-permute-start | bytes 786440 | tf_op jit(solution)/shard_map/ppermute | solution.py:242
  (22 other events, 74.4 us)
Sparse Core Ops, SparseCore 0:
  53.1 40.4 all-gather.2

commit v2 on v1

--- a/solution.py
+++ b/solution.py
@@ -67,10 +67,78 @@
     return jnp.concatenate(out, 0)
 
 
-def factor_kernel(s00, s10, s11, w, a, e):
-    a[0:T, 0:T] = 0.5 * (s00[...] + s00[...].T)
-    a[T:, 0:T] = s10[...]
-    a[T:, T:] = 0.5 * (s11[...] + s11[...].T)
+VMEM = pl.BlockSpec(memory_space=pltpu.VMEM)
+SMEM = pl.BlockSpec(memory_space=pltpu.SMEM)
+CHIPS = 16
+LEAD = 24
+
+
+def rows_of(chip, core):
+    return pl.ds(pl.multiple_of(16 * chip + 8 * core, 8), 8)
+
+
+def outward_kernel(where, pieces, first, got1, got2, got3, out, share):
+    for z in range(8):
+        for i, tile in enumerate((z, z + 8, z + 16, z + 24, 0, 1)):
+            out[z, 8 * i : 8 * i + 8] = pieces[tile]
+    share[...] = jnp.where(where[1] < 2, first[...], got1[...] + got2[...] + got3[...])
+
+
+def outward(where, pieces, first, got):
+    return pl.pallas_call(
+        outward_kernel,
+        out_shape=[jax.ShapeDtypeStruct((8, 48, T), F32), jax.ShapeDtypeStruct((T, T), F32)],
+        in_specs=[SMEM] + [VMEM] * 5,
+        out_specs=[VMEM] * 2,
+        compiler_params=pltpu.CompilerParams(vmem_limit_bytes=4 * MIB),
+        cost_estimate=pl.CostEstimate(flops=0, bytes_accessed=MIB, transcendentals=0),
+    )(where, pieces, first, *got)
+
+
+def inward_kernel(lines, tile, out, share):
+    head = jnp.concatenate([lines[0, 32:48], lines[1, 40:48]], axis=0)
+    for j in range(CHIPS):
+        out[j, 0:LEAD] = head
+        out[j, LEAD : LEAD + 32] = lines[0, 0:32]
+        out[j, LEAD + 32 :] = lines[1, 0:32]
+    share[...] = tile[...]
+
+
+def inward(lines, tile):
+    return pl.pallas_call(
+        inward_kernel,
+        out_shape=[jax.ShapeDtypeStruct((CHIPS, LEAD + 64, T), F32), jax.ShapeDtypeStruct((T, T), F32)],
+        in_specs=[VMEM] * 2,
+        out_specs=[VMEM, pl.BlockSpec((T, T), lambda: (0, 0))],
+        compiler_params=pltpu.CompilerParams(vmem_limit_bytes=4 * MIB),
+        cost_estimate=pl.CostEstimate(flops=0, bytes_accessed=2 * MIB, transcendentals=0),
+    )(lines, tile)
+
+
+def head_kernel(both, lead):
+    lead[...] = both[:, 0:LEAD]
+
+
+def head(both):
+    return pl.pallas_call(
+        head_kernel,
+        out_shape=jax.ShapeDtypeStruct((CHIPS, LEAD, T), F32),
+        in_specs=[VMEM],
+        out_specs=VMEM,
+        compiler_params=pltpu.CompilerParams(vmem_limit_bytes=4 * MIB),
+        cost_estimate=pl.CostEstimate(flops=0, bytes_accessed=MIB, transcendentals=0),
+    )(both)
+
+
+def factor_kernel(where, mine, other, w, a, e, tiles):
+    core = lax.rem(where[0], 2)
+    for j in range(CHIPS):
+        for t in range(3):
+            tiles[t, rows_of(j, core)] = mine[j, 8 * t : 8 * t + 8]
+            tiles[t, rows_of(j, 1 - core)] = other[j, 8 * t : 8 * t + 8]
+    a[0:T, 0:T] = 0.5 * (tiles[0] + tiles[0].T)
+    a[T:, 0:T] = tiles[1]
+    a[T:, T:] = 0.5 * (tiles[2] + tiles[2].T)
     w[...] = jnp.zeros_like(w)
     e[...] = jnp.zeros_like(e)
     for i in range(4):
@@ -88,17 +156,16 @@
             e[p:, 0:p] -= dot(low, w[o:p, 0:p])
 
 
-def factor(s00, s10, s11):
-    vmem = pl.BlockSpec(memory_space=pltpu.VMEM)
+def factor(where, mine, other):
     return pl.pallas_call(
         factor_kernel,
         out_shape=jax.ShapeDtypeStruct((2 * T, 2 * T), F32),
-        in_specs=[vmem] * 3,
-        out_specs=vmem,
-        scratch_shapes=[pltpu.VMEM((2 * T, 2 * T), F32)] * 2,
-        compiler_params=pltpu.CompilerParams(vmem_limit_bytes=16 * MIB),
-        cost_estimate=pl.CostEstimate(flops=10**9, bytes_accessed=2 * MIB, transcendentals=0),
-    )(s00, s10, s11)
+        in_specs=[SMEM, VMEM, VMEM],
+        out_specs=VMEM,
+        scratch_shapes=[pltpu.VMEM((2 * T, 2 * T), F32)] * 2 + [pltpu.VMEM((3, T, T), F32)],
+        compiler_params=pltpu.CompilerParams(vmem_limit_bytes=12 * MIB),
+        cost_estimate=pl.CostEstimate(flops=10**9, bytes_accessed=60 * MIB, transcendentals=0),
+    )(where, mine, other)
 
 
 def split(x):
@@ -106,11 +173,10 @@
     return high, (x - high.astype(F32)).astype(BF16)
 
 
-def update_kernel(where, a, p, g0, g1, g2, g3, h0, h1, h2, h3, w, out, mirror, y_high, y_low):
+def update_kernel(where, a, p0, p1, mine, other, w, out, mirror, y_high, y_low):
     r, c = where[0], where[1]
     m = pl.program_id(0)
     core = lax.rem(r, 2)
-    y = r // 8
 
     def solve(first, second):
         x0 = dot_t(first, w[0:T, 0:T])
@@ -119,10 +185,12 @@
 
     @pl.when(m == 0)
     def _():
-        for s, (g, h) in enumerate(((g0, h0), (g1, h1), (g2, h2), (g3, h3))):
-            n = lax.rem(y - s + 4, 4)
-            mirror[core, n] = g[...]
-            mirror[1 - core, n] = h[...]
+        for j in range(CHIPS):
+            for k in range(2):
+                for n in range(4):
+                    at = LEAD + 32 * k + 8 * n
+                    mirror[k, n, rows_of(j, core)] = mine[j, at : at + 8]
+                    mirror[k, n, rows_of(j, 1 - core)] = other[j, at : at + 8]
         for n in range(4):
             x0, x1 = solve(mirror[0, n], mirror[1, n])
             tile = n * 8 + c
@@ -133,7 +201,7 @@
                 y_high[n * T : (n + 1) * T, k * T : (k + 1) * T] = high
                 y_low[n * T : (n + 1) * T, k * T : (k + 1) * T] = low
 
-    x0, x1 = solve(p[:, 0].reshape(T, T), p[:, 1].reshape(T, T))
+    x0, x1 = solve(p0[0], p1[0])
     tile = m * 32 + r
     u0 = jnp.where(tile > 0, x0, 0.0)
     u1 = jnp.where(tile > 1, x1, 0.0)
@@ -160,90 +228,48 @@
             out[pl.ds(half * 4, T, stride=8), :] = x[:, half * B : (half + 1) * B]
 
 
-def update(where, a, p, g, h, w):
-    whole = pl.BlockSpec((T, T), lambda m: (0, 0))
+def update(where, a, panel, mine, other, w):
     return pl.pallas_call(
         update_kernel,
         grid=(4,),
         out_shape=jax.ShapeDtypeStruct(a.shape, F32),
         in_specs=[
-            pl.BlockSpec(memory_space=pltpu.SMEM),
+            SMEM,
             pl.BlockSpec((8 * T, B), lambda m: (m, 0)),
-            pl.BlockSpec((2, 2, B, T), lambda m: (m, 0, 0, 0)),
+            pl.BlockSpec((1, T, T), lambda m: (lax.rem(8 - m, 8), 0, 0)),
+            pl.BlockSpec((1, T, T), lambda m: (1 + m, 0, 0)),
         ]
-        + [whole] * 8
-        + [pl.BlockSpec((2 * T, 2 * T), lambda m: (0, 0))],
+        + [VMEM] * 3,
         out_specs=pl.BlockSpec((8 * T, B), lambda m: (m, 0)),
         scratch_shapes=[
             pltpu.VMEM((2, 4, T, T), F32),
             pltpu.VMEM((4 * T, 2 * T), BF16),
             pltpu.VMEM((4 * T, 2 * T), BF16),
         ],
-        compiler_params=pltpu.CompilerParams(vmem_limit_bytes=32 * MIB),
+        compiler_params=pltpu.CompilerParams(vmem_limit_bytes=52 * MIB),
         cost_estimate=pl.CostEstimate(flops=8 * 10**9, bytes_accessed=12 * MIB, transcendentals=0),
-    )(where, a, p, *g, *h, w)
-
-
-def device(r, c):
-    return r * 8 + c
-
-
-def send(x, pairs):
-    return lax.ppermute(x, ("row", "col"), [(device(*a), device(*b)) for a, b in pairs])
-
-
-def total(x, parts):
-    for part in parts:
-        x = x + part
-    return x
-
-
-def broadcast(x):
-    x = total(x, [send(x, [((0, 0), (8 * s, 0))]) for s in (1, 2, 3)])
-    x = total(x, [send(x, [((8 * y, 0), (8 * y + 2 * s, 0)) for y in range(4)]) for s in (1, 2, 3)])
-    chips = range(0, 32, 2)
-    x = total(x, [send(x, [((r, 0), (r, 2 * s)) for r in chips]) for s in (1, 2, 3)])
-    x = total(x, [send(x, [((r, z), (r, z + 1)) for r in chips for z in range(0, 8, 2)])])
-    return total(x, [send(x, [((r, z), (r + 1, z)) for r in chips for z in range(8)])])
+    )(where, a, panel, panel, mine, other, w)
 
 
 def per_device(matrix):
     r = lax.axis_index("row")
     c = lax.axis_index("col")
+    where = jnp.stack([r, c]).astype(jnp.int32)
     flat = matrix.reshape(4, T, 4, 2, B).transpose(0, 1, 3, 2, 4).reshape(4 * T * 8, B)
     column = matrix[:, :, 0, :]
-
     first = column[0]
-    origin = (r == 0) & (c == 0)
-    s00 = broadcast(jnp.where(origin, first, 0.0))
-    s10 = send(first, [((1, 0), (0, 0))])
-    s11 = send(first, [((1, 1), (0, 0))])
-    rest = broadcast(jnp.concatenate([s10, s11], axis=0))
-
-    chunks = column.reshape(8, B, T)
-    got = [lax.dynamic_index_in_dim(chunks, c, 0, keepdims=False)]
-    for s in range(1, 8):
-        piece = lax.dynamic_index_in_dim(chunks, lax.rem(c + s, 8), 0, keepdims=False)
-        got.append(lax.ppermute(piece, "col", [(0, s), (1, (1 + s) % 8)]))
-    got = jnp.stack(got)
-    mine = [lax.dynamic_index_in_dim(got, lax.rem(c + 8 - k, 8), 0, keepdims=False) for k in range(2)]
-    panel = lax.all_gather(jnp.stack(mine), "col", axis=0)
-
-    v = send(first, [((i, k), (i // 2 * 2 + k, i % 8)) for i in range(32) for k in range(2)])
-    lanes = [(y, z, k) for y in range(4) for z in range(8) for k in range(2)]
-    v = total(
-        v,
-        [
-            send(v, [((8 * y + z // 2 * 2 + k, z), (8 * y + (z // 2 + s) % 4 * 2 + k, z)) for y, z, k in lanes])
-            for s in (1, 2, 3)
-        ],
-    )
-    g = [v] + [lax.ppermute(v, "row", [(i, (i + 8 * s) % 32) for i in range(32)]) for s in (1, 2, 3)]
-    h = [lax.ppermute(t, "row", [(i, i ^ 1) for i in range(32)]) for t in g]
-
-    w = factor(s00, rest[:T], rest[T:])
-    where = jnp.stack([r, c]).astype(jnp.int32)
-    out = update(where, flat, panel, g, h, w)
+
+    got = [lax.ppermute(column[m], "col", [(0, 8 - m), (1, 1 + m)]) for m in (1, 2, 3)]
+    pieces = lax.all_to_all(first.reshape(32, 8, T), "row", 0, 0)
+    spread, tile = outward(where, pieces, first, got)
+    both, share = inward(lax.all_to_all(spread, "col", 0, 0), tile)
+    panel = lax.all_gather(share, "col", axis=0)
+
+    cores = [[2 * j + k for j in range(CHIPS)] for k in range(2)]
+    both = lax.all_to_all(both, "row", 0, 0, axis_index_groups=cores)
+    swap = [(i, i ^ 1) for i in range(32)]
+    w = factor(where, both, lax.ppermute(head(both), "row", swap))
+    out = update(where, flat, panel, both, lax.ppermute(both, "row", swap), w)
     return out.reshape(4, T, 2, 4, B).transpose(0, 1, 3, 2, 4).reshape(4, T, 4, T)
 
 

time: 183 us -> 133 us (0.73)
  starting transfers between devices: 105 us -> 23.8 us
  blocking collectives: 0 us -> 38.9 us
  local copies, waits for them, and re-layouts: 11 us -> 4.76 us
  Pallas kernels: 34.6 us -> 39.3 us
  waiting for transfers between devices: 15.6 us -> 11.9 us
    ppermute x42 -> x5, starting transfers between devices: 105 us -> 15.7 us  [the longest x3 10.9 us: per_device(): lax.ppermute(column[m], 'col', [(0, 8 - m), (1, 1 + m)])]
    all_to_all x0 -> x2, blocking collectives: none -> 38.9 us  [the longest x1 23.5 us: per_device(): both = lax.all_to_all(both, 'row', 0, 0, axis_index_groups=cores)]
    ppermute x42 -> x5, waiting for transfers between devices: 15.6 us -> 3.11 us  [the longest x1 3.1 us: per_device(): w = factor(where, both, lax.ppermute(head(both), 'row', swap))]
    all_to_all x0 -> x1, waiting for transfers between devices: none -> 8.77 us  [per_device(): pieces = lax.all_to_all(first.reshape(32, 8, T), 'row', 0, 0)]
    all_to_all x0 -> x1, starting transfers between devices: none -> 8.04 us  [per_device(): pieces = lax.all_to_all(first.reshape(32, 8, T), 'row', 0, 0)]
    unnamed x15 -> x8, local copies, waits for them, and re-layouts: 4.91 us -> 1.87 us
    pallas_call x1, Pallas kernels: 15.1 us -> 17.4 us  [update(): pl.pallas_call(update_kernel, grid=(4,), out_shape=jax.ShapeDtypeStruct(a...]
    pallas_call x0 -> x3, Pallas kernels: none -> 1.89 us  [the longest x1 1.05 us: outward(): pl.pallas_call(outward_kernel, out_shape=[jax.ShapeDtypeStruct((8, 48, T)...]
  transfers between devices with their start and end apart: 43 -> 7, of which waited for: 7 -> 2; matrix products, arithmetic and copies ran while one was open for 3% -> 1% of each run, Pallas kernels for 11% -> 15%
where the time goes in v2:
time: 133 us; the launch traced here: 132 us
  Pallas kernels  39.3 us (30%)
  blocking collectives  38.9 us (29%)
  starting transfers between devices  23.8 us (18%)
  between operations  13.5 us (10%)
  waiting for transfers between devices  11.9 us (9%)
  local copies, waits for them, and re-layouts  4.76 us (4%)
    all_to_all x1, blocking collectives, per_device(): both = lax.all_to_all(both, 'row', 0, 0, axis_index_groups=cores)  23.5 us
    pallas_call x1, Pallas kernels, factor(): pl.pallas_call(factor_kernel, out_shape=jax.ShapeDtypeStruct((2 * T, 2 *...  20 us
    pallas_call x1, Pallas kernels, update(): pl.pallas_call(update_kernel, grid=(4,), out_shape=jax.ShapeDtypeStruct(a...  17.4 us
    all_to_all x1, blocking collectives, per_device(): both, share = inward(lax.all_to_all(spread, 'col', 0, 0), tile)  15.4 us
    ppermute x3, starting transfers between devices, per_device(): lax.ppermute(column[m], 'col', [(0, 8 - m), (1, 1 + m)])  10.9 us
    all_to_all x1, waiting for transfers between devices, per_device(): pieces = lax.all_to_all(first.reshape(32, 8, T), 'row', 0, 0)  8.77 us
    all_to_all x1, starting transfers between devices, per_device(): pieces = lax.all_to_all(first.reshape(32, 8, T), 'row', 0, 0)  8.04 us
    ppermute x1, starting transfers between devices, per_device(): out = update(where, flat, panel, both, lax.ppermute(both, 'row', swap), w)  4.47 us
  transfers between devices with their start and end apart: 7, of which 2 were waited for; matrix products, arithmetic and copies ran while one was open for 1% of the time, Pallas kernels for 15%

profile of v2, /device:TPU:1, one launch (start us, length us, event | category | flops | bytes accessed | tf_op | source)
XLA Modules:
  0.0 132.3 jit_solution(17265371100283985054)
XLA Ops:
  6.5 2.9 %fusion = (f32[1,256,1,256]{3,2,1,0:T(1,128)S(1)}, f32[1,256,1,256]{3,2,1,0:T(1,128)S(1)}, f32[1,256,1,256]{3,2,1,0:T(1,128)S(1)}, f32[1,256,1,256]{3,2,1,0:T(1,128)S(1)}) fusion(f32[4,256,4,256]{3,2,1,0:T(4,128)} %param.1), kind=kLoop, calls=%fused_computation.6 | loop fusion | bytes 2097152 | tf_op jit(solution)/shard_map/slice | solution.py:262
  9.5 8.3 %collective-permute-start = (f32[256,256]{1,0:T(8,128)S(1)}, f32[256,256]{1,0:T(8,128)S(1)}, u32[]{:S(2)}, u32[]{:S(2)}) collective-permute-start(f32[256,256]{1,0:T(8,128)S(1)} %bitcast.28), channel_id=1, source_target_pairs={{0,7},{1,2},{8,15},{9,10},{16,23},{17,18},{24,31},{25,26},{32,39},... | collective-permute-start | bytes 786440 | tf_op jit(solution)/shard_map/ppermute | solution.py:262
  17.8 1.3 collective-permute-start.1
  19.2 1.3 collective-permute-start.2
  20.5 0.7 copy.20
  21.2 8.0 %all-to-all-start = ((f32[32,8,256]{2,1,0:T(8,128)}), f32[32,8,256]{2,1,0:T(8,128)S(1)}, u32[]{:S(2)}, u32[]{:S(2)}) async-start(f32[32,8,256]{2,1,0:T(8,128)} %bitcast.22.clone.2), calls=%async_computation | async-start | bytes 524288 | tf_op jit(solution)/shard_map/all_to_all | solution.py:263
  29.2 0.0 all-gather.3.cloned.1.call-start
  29.3 0.1 pad_add_fusion.where
  29.4 8.8 %all-to-all-done.pieces = f32[32,8,256]{2,1,0:T(8,128)S(1)} async-done(((f32[32,8,256]{2,1,0:T(8,128)}), f32[32,8,256]{2,1,0:T(8,128)S(1)}, u32[]{:S(2)}, u32[]{:S(2)}) %all-to-all-start) | async-done | bytes 262176 | tf_op jit(solution)/shard_map/all_to_all | solution.py:263
  38.1 0.0 collective-permute-done.1.got2
  38.1 0.0 collective-permute-done.2.got3
  38.2 1.1 shard_map.17
  39.2 15.4 %all_to_all.15.lines = f32[8,48,256]{2,1,0:T(8,128)S(1)} all-to-all(f32[8,48,256]{2,1,0:T(8,128)S(1)} %get-tuple-element.9), channel_id=1, replica_groups=mesh['row'=32,'col'=8] {'col'}, dimensions={0} | all-to-all | bytes 786432 | tf_op jit(solution)/shard_map/all_to_all | solution.py:265
  54.6 0.8 shard_map.18
  55.4 0.0 all-gather.3.cloned.1.call-update
  55.5 23.5 %all_to_all.16.both.mine = f32[16,88,256]{2,1,0:T(8,128)S(1)} all-to-all(f32[16,88,256]{2,1,0:T(8,128)S(1)} %get-tuple-element.12), channel_id=1, replica_groups={{0,16,32,48,64,80,96,112,128,144,160,176,192,208,224,240},{8,24,40,56,7..., dimensions={0} | all-to-all | bytes 2883584 | tf_op jit(solution)/shard_map/all_to_all | solution.py:269
  79.0 4.5 %collective-permute-start.3 = (f32[16,88,256]{2,1,0:T(8,128)S(1)}, f32[16,88,256]{2,1,0:T(8,128)S(1)}, u32[]{:S(2)}, u32[]{:S(2)}) collective-permute-start(f32[16,88,256]{2,1,0:T(8,128)S(1)} %all_to_all.16.both.mine), channel_id=1, source_target_pairs={{0,8},{8,0},{16,24},{24,16},{32,40},{40,32},{48,56},{56,48},{64,72... | collective-permute-start | bytes 4325384 | tf_op jit(solution)/shard_map/ppermute | solution.py:272
  83.5 0.3 collective-permute-start.4
  83.7 3.1 %collective-permute-done.4.other = f32[16,24,256]{2,1,0:T(8,128)S(1)} collective-permute-done((f32[16,24,256]{2,1,0:T(8,128)S(1)}, f32[16,24,256]{2,1,0:T(8,128)S(1)}, u32[]{:S(2)}, u32[]{:S(2)}) %collective-permute-start.4) | collective-permute-done | bytes 393248 | tf_op jit(solution)/shard_map/ppermute | solution.py:271
  86.8 20.0 %shard_map.20.w = f32[512,512]{1,0:T(8,128)S(1)} custom-call(s32[2]{0:T(128)S(1)} %pad_add_fusion.where, f32[16,88,256]{2,1,0:T(8,128)S(1)} %all_to_all.16.both.mine, f32[16,24,256]{2,1,0:T(8,128)S(1)} %collective-permute-done.4.other), custom_call_target="tpu_custom_call" | custom-call | flops 1000000000 | bytes 62914560 | tf_op jit(solution)/shard_map/pallas_call | solution.py:160
  106.9 0.0 collective-permute-done.3.other
  106.9 0.0 all-gather.3.cloned.1.call-done
  106.9 1.1 copy-done.1
  108.0 17.4 %shard_map.21 = f32[8192,128]{1,0:T(8,128)} custom-call(s32[2]{0:T(128)S(1)} %pad_add_fusion.where, f32[8192,128]{1,0:T(8,128)} %bitcast.27, f32[8,256,256]{2,1,0:T(8,128)} %bitcast.31, f32[8,256,256]{2,1,0:T(8,128)} %bitcast.32, f32[16,88,256]{2,1,0:T(8,128)} %copy-done, f32[16,88,256]{2,1,0:T(8,128)} %copy-done.1, f32[512,512]{1,0:T(8,128)S(1)} %shard_map.20.w), custom_call_target="tpu_custom_call" | custom-call | flops 8000000000 | bytes 12582912 | tf_op jit(solution)/shard_map/pallas_call | solution.py:232
  (8 shorter events, 0.1 us)
Async XLA Ops:
  9.5 28.7 %collective-permute-start = (f32[256,256]{1,0:T(8,128)S(1)}, f32[256,256]{1,0:T(8,128)S(1)}, u32[]{:S(2)}, u32[]{:S(2)}) collective-permute-start(f32[256,256]{1,0:T(8,128)S(1)} %bitcast.28), channel_id=1, source_target_pairs={{0,7},{1,2},{8,15},{9,10},{16,23},{17,18},{24,31},{25,26},{32,39},... | collective-permute-start | bytes 786440 | tf_op jit(solution)/shard_map/ppermute | solution.py:262
  17.8 20.3 %collective-permute-start.1 = (f32[256,256]{1,0:T(8,128)S(1)}, f32[256,256]{1,0:T(8,128)S(1)}, u32[]{:S(2)}, u32[]{:S(2)}) collective-permute-start(f32[256,256]{1,0:T(8,128)S(1)} %bitcast.29), channel_id=1, source_target_pairs={{0,6},{1,3},{8,14},{9,11},{16,22},{17,19},{24,30},{25,27},{32,38},... | collective-permute-start | bytes 786440 | tf_op jit(solution)/shard_map/ppermute | solution.py:262
  19.2 19.0 %collective-permute-start.2 = (f32[256,256]{1,0:T(8,128)S(1)}, f32[256,256]{1,0:T(8,128)S(1)}, u32[]{:S(2)}, u32[]{:S(2)}) collective-permute-start(f32[256,256]{1,0:T(8,128)S(1)} %bitcast.30), channel_id=1, source_target_pairs={{0,5},{1,4},{8,13},{9,12},{16,21},{17,20},{24,29},{25,28},{32,37},... | collective-permute-start | bytes 786440 | tf_op jit(solution)/shard_map/ppermute | solution.py:262
  21.2 16.9 %all-to-all-start = ((f32[32,8,256]{2,1,0:T(8,128)}), f32[32,8,256]{2,1,0:T(8,128)S(1)}, u32[]{:S(2)}, u32[]{:S(2)}) async-start(f32[32,8,256]{2,1,0:T(8,128)} %bitcast.22.clone.2), calls=%async_computation | async-start | bytes 524288 | tf_op jit(solution)/shard_map/all_to_all | solution.py:263
  29.2 77.7 %all-gather.3.cloned.1.call-start = ((), (), s32[]{:S(2)}) async-start(), calls=%async_computation.3 | async-start | bytes 2359296 | tf_op jit(solution)/shard_map/all_gather | solution.py:266
  79.0 27.9 %copy-start = (f32[16,88,256]{2,1,0:T(8,128)}, f32[16,88,256]{2,1,0:T(8,128)S(1)}, u32[]{:S(2)}) copy-start(f32[16,88,256]{2,1,0:T(8,128)S(1)} %all_to_all.16.both.mine) | copy-start | bytes 4325380
  79.0 27.9 %collective-permute-start.3 = (f32[16,88,256]{2,1,0:T(8,128)S(1)}, f32[16,88,256]{2,1,0:T(8,128)S(1)}, u32[]{:S(2)}, u32[]{:S(2)}) collective-permute-start(f32[16,88,256]{2,1,0:T(8,128)S(1)} %all_to_all.16.both.mine), channel_id=1, source_target_pairs={{0,8},{8,0},{16,24},{24,16},{32,40},{40,32},{48,56},{56,48},{64,72... | collective-permute-start | bytes 4325384 | tf_op jit(solution)/shard_map/ppermute | solution.py:272
  83.5 3.4 %collective-permute-start.4 = (f32[16,24,256]{2,1,0:T(8,128)S(1)}, f32[16,24,256]{2,1,0:T(8,128)S(1)}, u32[]{:S(2)}, u32[]{:S(2)}) collective-permute-start(f32[16,24,256]{2,1,0:T(8,128)S(1)} %shard_map.19), channel_id=1, source_target_pairs={{0,8},{8,0},{16,24},{24,16},{32,40},{40,32},{48,56},{56,48},{64,72... | collective-permute-start | bytes 1179656 | tf_op jit(solution)/shard_map/ppermute | solution.py:271
  106.9 1.1 copy-start.1
Sparse Core Ops, SparseCore 0:
  55.6 35.5 all-gather.2

commit v3 on v2

--- a/solution.py
+++ b/solution.py
@@ -96,9 +96,9 @@
 
 
 def inward_kernel(lines, tile, out, share):
-    head = jnp.concatenate([lines[0, 32:48], lines[1, 40:48]], axis=0)
     for j in range(CHIPS):
-        out[j, 0:LEAD] = head
+        out[j, 0:16] = lines[0, 32:48]
+        out[j, 16:LEAD] = lines[1, 40:48]
         out[j, LEAD : LEAD + 32] = lines[0, 0:32]
         out[j, LEAD + 32 :] = lines[1, 0:32]
     share[...] = tile[...]
@@ -107,7 +107,7 @@
 def inward(lines, tile):
     return pl.pallas_call(
         inward_kernel,
-        out_shape=[jax.ShapeDtypeStruct((CHIPS, LEAD + 64, T), F32), jax.ShapeDtypeStruct((T, T), F32)],
+        out_shape=[jax.ShapeDtypeStruct((CHIPS, LEAD + 64, T), F32), square(T)],
         in_specs=[VMEM] * 2,
         out_specs=[VMEM, pl.BlockSpec((T, T), lambda: (0, 0))],
         compiler_params=pltpu.CompilerParams(vmem_limit_bytes=4 * MIB),
@@ -130,7 +130,7 @@
     )(both)
 
 
-def factor_kernel(where, mine, other, w, a, e, tiles):
+def first_kernel(where, mine, other, both, w, e_low, a_low, same, a, e, tiles):
     core = lax.rem(where[0], 2)
     for j in range(CHIPS):
         for t in range(3):
@@ -141,31 +141,60 @@
     a[T:, T:] = 0.5 * (tiles[2] + tiles[2].T)
     w[...] = jnp.zeros_like(w)
     e[...] = jnp.zeros_like(e)
-    for i in range(4):
+    for i in range(2):
         o = i * B
         p = o + B
         part = leaf(a[o:p, o:p])
         w[o:p, o:p] = part
         if i:
             w[o:p, 0:o] = dot(part, e[o:p, 0:o])
-        if i < 3:
-            low = dot_t(a[p:, o:p], part)
-            for j in range(i + 1, 4):
-                r = (j - i - 1) * B
-                a[j * B :, j * B : (j + 1) * B] -= dot_t(low[r:], low[r : r + B])
-            e[p:, 0:p] -= dot(low, w[o:p, 0:p])
-
-
-def factor(where, mine, other):
-    return pl.pallas_call(
-        factor_kernel,
-        out_shape=jax.ShapeDtypeStruct((2 * T, 2 * T), F32),
-        in_specs=[SMEM, VMEM, VMEM],
-        out_specs=VMEM,
-        scratch_shapes=[pltpu.VMEM((2 * T, 2 * T), F32)] * 2 + [pltpu.VMEM((3, T, T), F32)],
+        low = dot_t(a[p:, o:p], part)
+        for j in range(i + 1, 4):
+            r = (j - i - 1) * B
+            a[j * B :, j * B : (j + 1) * B] -= dot_t(low[r:], low[r : r + B])
+        e[p:, 0:p] -= dot(low, w[o:p, 0:p])
+    e_low[...] = e[T:, :]
+    a_low[...] = a[T:, T:]
+
+
+def second_kernel(a, e_low, w, w_low):
+    top = leaf(a[0:B, 0:B])
+    low = dot_t(a[B:, 0:B], top)
+    end = leaf(a[B:, B:] - dot_t(low, low))
+    w[0:B, 0:B] = top
+    w[0:B, B:] = jnp.zeros((B, B), F32)
+    w[B:, 0:B] = -dot(end, dot(low, top))
+    w[B:, B:] = end
+    w_low[...] = dot(w[...], e_low[...])
+
+
+def square(n):
+    return jax.ShapeDtypeStruct((n, n), F32)
+
+
+def first_factor(where, mine, other, both):
+    far = pl.BlockSpec(memory_space=pl.ANY)
+    return pl.pallas_call(
+        first_kernel,
+        out_shape=[square(T)] * 3 + [jax.ShapeDtypeStruct(both.shape, F32)],
+        in_specs=[SMEM, VMEM, VMEM, far],
+        out_specs=[VMEM] * 3 + [far],
+        input_output_aliases={3: 3},
+        scratch_shapes=[pltpu.VMEM((2 * T, 2 * T), F32), pltpu.VMEM((2 * T, T), F32), pltpu.VMEM((3, T, T), F32)],
         compiler_params=pltpu.CompilerParams(vmem_limit_bytes=12 * MIB),
-        cost_estimate=pl.CostEstimate(flops=10**9, bytes_accessed=60 * MIB, transcendentals=0),
-    )(where, mine, other)
+        cost_estimate=pl.CostEstimate(flops=10**9, bytes_accessed=40 * MIB, transcendentals=0),
+    )(where, mine, other, both)
+
+
+def second_factor(a, e_low):
+    return pl.pallas_call(
+        second_kernel,
+        out_shape=[square(T)] * 2,
+        in_specs=[VMEM] * 2,
+        out_specs=[VMEM] * 2,
+        compiler_params=pltpu.CompilerParams(vmem_limit_bytes=12 * MIB),
+        cost_estimate=pl.CostEstimate(flops=10**9, bytes_accessed=40 * MIB, transcendentals=0),
+    )(a, e_low)
 
 
 def split(x):
@@ -173,82 +202,121 @@
     return high, (x - high.astype(F32)).astype(BF16)
 
 
-def update_kernel(where, a, p0, p1, mine, other, w, out, mirror, y_high, y_low):
+def thirds(x):
+    high = x.astype(BF16)
+    rest = x - high.astype(F32)
+    middle = rest.astype(BF16)
+    return high, middle, (rest - middle.astype(F32)).astype(BF16)
+
+
+def mul(u, v):
+    return lax.dot_general(u, v, (((1,), (1,)), ((), ())), preferred_element_type=F32)
+
+
+def lay(ref, at, x, order):
+    parts = thirds(x)
+    for i, part in enumerate(order):
+        ref[:, at + i * T : at + (i + 1) * T] = parts[part]
+
+
+LEFT = (0, 0, 1, 1, 0, 2)
+RIGHT = (0, 1, 0, 1, 2, 0)
+SIX = 6 * T
+STEP = 256
+
+
+def update_kernel(where, a, p, mine, other, w00, w10, w11, out, buf, panel, mirror, x_out, left, right, x_cat, y_cat, sem_a, sem_p, sem_out):
     r, c = where[0], where[1]
-    m = pl.program_id(0)
     core = lax.rem(r, 2)
-
-    def solve(first, second):
-        x0 = dot_t(first, w[0:T, 0:T])
-        x1 = dot_t(first, w[T:, 0:T]) + dot_t(second, w[T:, T:])
-        return x0, x1
-
-    @pl.when(m == 0)
-    def _():
-        for j in range(CHIPS):
-            for k in range(2):
-                for n in range(4):
-                    at = LEAD + 32 * k + 8 * n
-                    mirror[k, n, rows_of(j, core)] = mine[j, at : at + 8]
-                    mirror[k, n, rows_of(j, 1 - core)] = other[j, at : at + 8]
+    n_half = 4 * T * 8 // 2
+    loads = [pltpu.make_async_copy(a.at[pl.ds(i * n_half, n_half)], buf.at[pl.ds(i * n_half, n_half)], sem_a.at[i]) for i in range(2)]
+    fetch = pltpu.make_async_copy(p, panel, sem_p)
+    fetch.start()
+    for load in loads:
+        load.start()
+    for i, t in enumerate((w00, w10, w11)):
+        lay(right, i * SIX, t[...], RIGHT)
+
+    def solve(first, second, stride, start, cat, order, keep):
+        lay(left, 0, first, LEFT)
+        lay(left, SIX, second, LEFT)
+        for i in range(0, 4 * T, STEP):
+            rows = slice(i, i + STEP)
+            x0 = mul(left[rows, 0:SIX], right[:, 0:SIX])
+            x1 = mul(left[rows], right[:, SIX:])
+            if keep:
+                x_out[rows] = jnp.where(c == 0, x0, x1)
+            tile = (lax.broadcasted_iota(jnp.int32, (STEP, 1), 0) + i) // T * stride + start
+            for k, x in enumerate((x0, x1)):
+                parts = split(jnp.where(tile > k, x, 0.0))
+                for j, part in enumerate(order):
+                    at = (2 * j + k) * T
+                    cat[rows, at : at + T] = parts[part]
+
+    for j in range(CHIPS):
+        for k in range(2):
+            for n in range(4):
+                at = LEAD + 32 * k + 8 * n
+                mirror[k, n, rows_of(j, core)] = mine[j, at : at + 8]
+                mirror[k, n, rows_of(j, 1 - core)] = other[j, at : at + 8]
+    solve(mirror[0].reshape(4 * T, T), mirror[1].reshape(4 * T, T), 8, c, y_cat, (0, 0, 1), False)
+    fetch.wait()
+    first = jnp.concatenate([panel[0], panel[7], panel[6], panel[5]], axis=0)
+    solve(first, panel[1:5].reshape(4 * T, T), 32, r, x_cat, (0, 1, 0), True)
+
+    rows = 2 * T
+    stores = []
+    for i in range(2):
+        loads[i].wait()
+        span = slice(i * rows, (i + 1) * rows)
         for n in range(4):
-            x0, x1 = solve(mirror[0, n], mirror[1, n])
-            tile = n * 8 + c
-            x0 = jnp.where(tile > 0, x0, 0.0)
-            x1 = jnp.where(tile > 1, x1, 0.0)
-            for k, x in enumerate((x0, x1)):
-                high, low = split(x)
-                y_high[n * T : (n + 1) * T, k * T : (k + 1) * T] = high
-                y_low[n * T : (n + 1) * T, k * T : (k + 1) * T] = low
-
-    x0, x1 = solve(p0[0], p1[0])
-    tile = m * 32 + r
-    u0 = jnp.where(tile > 0, x0, 0.0)
-    u1 = jnp.where(tile > 1, x1, 0.0)
-    x_high, x_low = split(jnp.concatenate([u0, u1], axis=1))
-
-    def mul(u, v):
-        return lax.dot_general(u, v, (((1,), (1,)), ((), ())), preferred_element_type=F32)
-
-    for n in range(4):
-        span = slice(n * T, (n + 1) * T)
-        product = mul(x_high, y_high[span]) + mul(x_high, y_low[span]) + mul(x_low, y_high[span])
-        for half in range(2):
-            at = pl.ds(half * 4 + n, T, stride=8)
-            out[at, :] = a[at, :] - product[:, half * B : (half + 1) * B]
-
-    @pl.when(c < 2)
-    def _():
-        row = lax.broadcasted_iota(jnp.int32, (T, T), 0)
-        col = lax.broadcasted_iota(jnp.int32, (T, T), 1)
-        x = jnp.where(c == 0, x0, x1)
-        keep = (tile > c) | ((tile == c) & (row >= col))
-        x = jnp.where(keep, x, 0.0)
-        for half in range(2):
-            out[pl.ds(half * 4, T, stride=8), :] = x[:, half * B : (half + 1) * B]
+            cols = slice(n * T, (n + 1) * T)
+            product = mul(x_cat[span], y_cat[cols])
+            for half in range(2):
+                at = pl.ds(i * n_half + half * 4 + n, rows, stride=8)
+                buf[at, :] = buf[at, :] - product[:, half * B : (half + 1) * B]
+
+        @pl.when(c < 2)
+        def _():
+            row = lax.broadcasted_iota(jnp.int32, (rows, T), 0) + i * rows
+            col = lax.broadcasted_iota(jnp.int32, (rows, T), 1)
+            tile = row // T * 32 + r
+            keep = (tile > c) | ((tile == c) & (lax.rem(row, T) >= col))
+            x = jnp.where(keep, x_out[span], 0.0)
+            for half in range(2):
+                buf[pl.ds(i * n_half + half * 4, rows, stride=8), :] = x[:, half * B : (half + 1) * B]
+
+        at = pl.ds(i * n_half, n_half)
+        stores.append(pltpu.make_async_copy(buf.at[at], out.at[at], sem_out.at[i]))
+        stores[i].start()
+    for store in stores:
+        store.wait()
 
 
 def update(where, a, panel, mine, other, w):
+    hbm = pl.BlockSpec(memory_space=pltpu.HBM)
+    a, panel = (pltpu.with_memory_space_constraint(t, pltpu.HBM) for t in (a, panel))
     return pl.pallas_call(
         update_kernel,
-        grid=(4,),
         out_shape=jax.ShapeDtypeStruct(a.shape, F32),
-        in_specs=[
-            SMEM,
-            pl.BlockSpec((8 * T, B), lambda m: (m, 0)),
-            pl.BlockSpec((1, T, T), lambda m: (lax.rem(8 - m, 8), 0, 0)),
-            pl.BlockSpec((1, T, T), lambda m: (1 + m, 0, 0)),
-        ]
-        + [VMEM] * 3,
-        out_specs=pl.BlockSpec((8 * T, B), lambda m: (m, 0)),
+        in_specs=[SMEM, hbm, hbm] + [VMEM] * 5,
+        out_specs=hbm,
         scratch_shapes=[
+            pltpu.VMEM((4 * T * 8, B), F32),
+            pltpu.VMEM((8, T, T), F32),
             pltpu.VMEM((2, 4, T, T), F32),
-            pltpu.VMEM((4 * T, 2 * T), BF16),
-            pltpu.VMEM((4 * T, 2 * T), BF16),
+            pltpu.VMEM((4 * T, T), F32),
+            pltpu.VMEM((4 * T, 2 * SIX), BF16),
+            pltpu.VMEM((T, 3 * SIX), BF16),
+            pltpu.VMEM((4 * T, SIX), BF16),
+            pltpu.VMEM((4 * T, SIX), BF16),
+            pltpu.SemaphoreType.DMA((2,)),
+            pltpu.SemaphoreType.DMA,
+            pltpu.SemaphoreType.DMA((2,)),
         ],
-        compiler_params=pltpu.CompilerParams(vmem_limit_bytes=52 * MIB),
+        compiler_params=pltpu.CompilerParams(vmem_limit_bytes=38 * MIB),
         cost_estimate=pl.CostEstimate(flops=8 * 10**9, bytes_accessed=12 * MIB, transcendentals=0),
-    )(where, a, panel, panel, mine, other, w)
+    )(where, a, panel, mine, other, *w)
 
 
 def per_device(matrix):
@@ -266,10 +334,12 @@
     panel = lax.all_gather(share, "col", axis=0)
 
     cores = [[2 * j + k for j in range(CHIPS)] for k in range(2)]
+    swap = [(i, i ^ 1) for i in range(32)]
     both = lax.all_to_all(both, "row", 0, 0, axis_index_groups=cores)
-    swap = [(i, i ^ 1) for i in range(32)]
-    w = factor(where, both, lax.ppermute(head(both), "row", swap))
-    out = update(where, flat, panel, both, lax.ppermute(both, "row", swap), w)
+    lead = head(both)
+    w00, e_low, a_low, both = first_factor(where, lead, lax.ppermute(lead, "row", swap), both)
+    w11, w10 = second_factor(a_low, e_low)
+    out = update(where, flat, panel, both, lax.ppermute(both, "row", swap), (w00, w10, w11))
     return out.reshape(4, T, 2, 4, B).transpose(0, 1, 3, 2, 4).reshape(4, T, 4, T)
 
 

time: 133 us -> 129 us (0.970)
  Pallas kernels: 39.3 us -> 36.1 us
  waiting for transfers between devices: 11.9 us -> 10.1 us
    pallas_call x2 -> x3, Pallas kernels: 37.4 us -> 34.2 us  [the longest x1 14.2 us: update(): pl.pallas_call(update_kernel, out_shape=jax.ShapeDtypeStruct(a.shape, F32...]
    ppermute x2, waiting for transfers between devices: 3.1 us -> 1.35 us  [the longest x1 1.35 us: per_device(): lax.ppermute(lead, 'row', swap)]
  transfers between devices with their start and end apart: 7 -> 7, of which waited for: 2 -> 2; matrix products, arithmetic and copies ran while one was open for 1% -> 1% of each run, Pallas kernels for 15% -> 16%
where the time goes in v3:
time: 129 us; the launch traced here: 128 us
  blocking collectives  38.9 us (30%)
  Pallas kernels  36.1 us (28%)
  starting transfers between devices  24.2 us (19%)
  between operations  13.5 us (10%)
  waiting for transfers between devices  10.1 us (8%)
  local copies, waits for them, and re-layouts  5.33 us (4%)
    all_to_all x1, blocking collectives, per_device(): both = lax.all_to_all(both, 'row', 0, 0, axis_index_groups=cores)  23.5 us
    all_to_all x1, blocking collectives, per_device(): both, share = inward(lax.all_to_all(spread, 'col', 0, 0), tile)  15.4 us
    pallas_call x1, Pallas kernels, update(): pl.pallas_call(update_kernel, out_shape=jax.ShapeDtypeStruct(a.shape, F32...  14.2 us
    ppermute x3, starting transfers between devices, per_device(): lax.ppermute(column[m], 'col', [(0, 8 - m), (1, 1 + m)])  10.9 us
    pallas_call x1, Pallas kernels, first_factor(): pl.pallas_call(first_kernel, out_shape=[square(T)] * 3 + [jax.ShapeDtypeS...  10.7 us
    pallas_call x1, Pallas kernels, second_factor(): pl.pallas_call(second_kernel, out_shape=[square(T)] * 2, in_specs=[VMEM]...  9.37 us
    all_to_all x1, waiting for transfers between devices, per_device(): pieces = lax.all_to_all(first.reshape(32, 8, T), 'row', 0, 0)  8.77 us
    all_to_all x1, starting transfers between devices, per_device(): pieces = lax.all_to_all(first.reshape(32, 8, T), 'row', 0, 0)  8.04 us
  transfers between devices with their start and end apart: 7, of which 2 were waited for; matrix products, arithmetic and copies ran while one was open for 1% of the time, Pallas kernels for 16%

profile of v3, /device:TPU:1, one launch (start us, length us, event | category | flops | bytes accessed | tf_op | source)
XLA Modules:
  0.0 128.3 jit_solution(14932309147602116736)
XLA Ops:
  6.5 2.9 %fusion = (f32[1,256,1,256]{3,2,1,0:T(1,128)S(1)}, f32[1,256,1,256]{3,2,1,0:T(1,128)S(1)}, f32[1,256,1,256]{3,2,1,0:T(1,128)S(1)}, f32[1,256,1,256]{3,2,1,0:T(1,128)S(1)}) fusion(f32[4,256,4,256]{3,2,1,0:T(4,128)} %param.1), kind=kLoop, calls=%fused_computation.6 | loop fusion | bytes 2097152 | tf_op jit(solution)/shard_map/slice | solution.py:330
  9.5 8.3 %collective-permute-start = (f32[256,256]{1,0:T(8,128)S(1)}, f32[256,256]{1,0:T(8,128)S(1)}, u32[]{:S(2)}, u32[]{:S(2)}) collective-permute-start(f32[256,256]{1,0:T(8,128)S(1)} %bitcast.28), channel_id=1, source_target_pairs={{0,7},{1,2},{8,15},{9,10},{16,23},{17,18},{24,31},{25,26},{32,39},... | collective-permute-start | bytes 786440 | tf_op jit(solution)/shard_map/ppermute | solution.py:330
  17.8 1.3 %collective-permute-start.1 = (f32[256,256]{1,0:T(8,128)S(1)}, f32[256,256]{1,0:T(8,128)S(1)}, u32[]{:S(2)}, u32[]{:S(2)}) collective-permute-start(f32[256,256]{1,0:T(8,128)S(1)} %bitcast.29), channel_id=1, source_target_pairs={{0,6},{1,3},{8,14},{9,11},{16,22},{17,19},{24,30},{25,27},{32,38},... | collective-permute-start | bytes 786440 | tf_op jit(solution)/shard_map/ppermute | solution.py:330
  19.2 1.3 %collective-permute-start.2 = (f32[256,256]{1,0:T(8,128)S(1)}, f32[256,256]{1,0:T(8,128)S(1)}, u32[]{:S(2)}, u32[]{:S(2)}) collective-permute-start(f32[256,256]{1,0:T(8,128)S(1)} %bitcast.30), channel_id=1, source_target_pairs={{0,5},{1,4},{8,13},{9,12},{16,21},{17,20},{24,29},{25,28},{32,37},... | collective-permute-start | bytes 786440 | tf_op jit(solution)/shard_map/ppermute | solution.py:330
  20.5 0.7 copy.21
  21.2 8.0 %all-to-all-start = ((f32[32,8,256]{2,1,0:T(8,128)}), f32[32,8,256]{2,1,0:T(8,128)S(1)}, u32[]{:S(2)}, u32[]{:S(2)}) async-start(f32[32,8,256]{2,1,0:T(8,128)} %bitcast.22.clone.2), calls=%async_computation | async-start | bytes 524288 | tf_op jit(solution)/shard_map/all_to_all | solution.py:331
  29.2 0.0 all-gather.3.cloned.1.call-start
  29.3 0.1 pad_add_fusion.where
  29.4 8.8 %all-to-all-done.pieces = f32[32,8,256]{2,1,0:T(8,128)S(1)} async-done(((f32[32,8,256]{2,1,0:T(8,128)}), f32[32,8,256]{2,1,0:T(8,128)S(1)}, u32[]{:S(2)}, u32[]{:S(2)}) %all-to-all-start) | async-done | bytes 262176 | tf_op jit(solution)/shard_map/all_to_all | solution.py:331
  38.1 0.0 collective-permute-done.2.got3
  38.2 1.1 shard_map.17
  39.2 15.4 %all_to_all.15.lines = f32[8,48,256]{2,1,0:T(8,128)S(1)} all-to-all(f32[8,48,256]{2,1,0:T(8,128)S(1)} %get-tuple-element.15), channel_id=1, replica_groups=mesh['row'=32,'col'=8] {'col'}, dimensions={0} | all-to-all | bytes 786432 | tf_op jit(solution)/shard_map/all_to_all | solution.py:333
  54.6 0.8 shard_map.18
  55.4 0.0 all-gather.3.cloned.1.call-update
  55.5 23.5 %all_to_all.16.both = f32[16,88,256]{2,1,0:T(8,128)S(1)} all-to-all(f32[16,88,256]{2,1,0:T(8,128)S(1)} %get-tuple-element.18), channel_id=1, replica_groups={{0,16,32,48,64,80,96,112,128,144,160,176,192,208,224,240},{8,24,40,56,7..., dimensions={0} | all-to-all | bytes 2883584 | tf_op jit(solution)/shard_map/all_to_all | solution.py:338
  79.0 4.6 %collective-permute-start.3 = (f32[16,24,256]{2,1,0:T(8,128)S(1)}, f32[16,24,256]{2,1,0:T(8,128)S(1)}, u32[]{:S(2)}, u32[]{:S(2)}) collective-permute-start(f32[16,24,256]{2,1,0:T(8,128)S(1)} %shard_map.19.mine), channel_id=1, source_target_pairs={{0,8},{8,0},{16,24},{24,16},{32,40},{40,32},{48,56},{56,48},{64,72... | collective-permute-start | bytes 1179656 | tf_op jit(solution)/shard_map/ppermute | solution.py:340
  83.5 1.3 %collective-permute-done.3.other = f32[16,24,256]{2,1,0:T(8,128)S(1)} collective-permute-done((f32[16,24,256]{2,1,0:T(8,128)S(1)}, f32[16,24,256]{2,1,0:T(8,128)S(1)}, u32[]{:S(2)}, u32[]{:S(2)}) %collective-permute-start.3) | collective-permute-done | bytes 393248 | tf_op jit(solution)/shard_map/ppermute | solution.py:340
  84.9 10.7 %shard_map.20 = (f32[256,256]{1,0:T(8,128)S(1)}, f32[256,256]{1,0:T(8,128)S(1)}, f32[256,256]{1,0:T(8,128)S(1)}, f32[16,88,256]{2,1,0:T(8,128)S(1)}) custom-call(s32[2]{0:T(128)S(1)} %pad_add_fusion.where, f32[16,24,256]{2,1,0:T(8,128)S(1)} %shard_map.19.mine, f32[16,24,256]{2,1,0:T(8,128)S(1)} %collective-permute-done.3.other, ...), custom_call_target="tpu_custom_call", output_to_operand_aliasing={{3}: (3, {})} | custom-call | flops 1000000000 | bytes 41943040 | tf_op jit(solution)/shard_map/pallas_call | solution.py:177
  95.6 0.6 collective-permute-start.4
  96.2 9.4 %shard_map.21 = (f32[256,256]{1,0:T(8,128)S(1)}, f32[256,256]{1,0:T(8,128)S(1)}) custom-call(f32[256,256]{1,0:T(8,128)S(1)} %get-tuple-element.21.a, f32[256,256]{1,0:T(8,128)S(1)} %get-tuple-element.22.e_low), custom_call_target="tpu_custom_call" | custom-call | flops 1000000000 | bytes 41943040 | tf_op jit(solution)/shard_map/pallas_call | solution.py:190
  105.6 0.7 copy-done
  106.3 0.0 collective-permute-done.4.other
  106.3 0.9 copy-done.1
  107.3 14.2 %shard_map.22 = f32[8192,128]{1,0:T(8,128)} custom-call(s32[2]{0:T(128)S(1)} %pad_add_fusion.where, f32[8192,128]{1,0:T(8,128)} %bitcast.27, f32[8,256,256]{2,1,0:T(8,128)} %bitcast.31, f32[16,88,256]{2,1,0:T(8,128)S(1)} %get-tuple-element.19.mine, f32[16,88,256]{2,1,0:T(8,128)S(1)} %collective-permute-done.4.other, f32[256,256]{1,0:T(8,128)S(1)} %get-tuple-element.20.w00, ...), custom_call_target="tpu_custom_call" | custom-call | flops 8000000000 | bytes 12582912 | tf_op jit(solution)/shard_map/pallas_call | solution.py:299
  (9 shorter events, 0.1 us)
Async XLA Ops:
  9.5 28.7 %collective-permute-start = (f32[256,256]{1,0:T(8,128)S(1)}, f32[256,256]{1,0:T(8,128)S(1)}, u32[]{:S(2)}, u32[]{:S(2)}) collective-permute-start(f32[256,256]{1,0:T(8,128)S(1)} %bitcast.28), channel_id=1, source_target_pairs={{0,7},{1,2},{8,15},{9,10},{16,23},{17,18},{24,31},{25,26},{32,39},... | collective-permute-start | bytes 786440 | tf_op jit(solution)/shard_map/ppermute | solution.py:330
  17.8 20.3 %collective-permute-start.1 = (f32[256,256]{1,0:T(8,128)S(1)}, f32[256,256]{1,0:T(8,128)S(1)}, u32[]{:S(2)}, u32[]{:S(2)}) collective-permute-start(f32[256,256]{1,0:T(8,128)S(1)} %bitcast.29), channel_id=1, source_target_pairs={{0,6},{1,3},{8,14},{9,11},{16,22},{17,19},{24,30},{25,27},{32,38},... | collective-permute-start | bytes 786440 | tf_op jit(solution)/shard_map/ppermute | solution.py:330
  19.2 19.0 %collective-permute-start.2 = (f32[256,256]{1,0:T(8,128)S(1)}, f32[256,256]{1,0:T(8,128)S(1)}, u32[]{:S(2)}, u32[]{:S(2)}) collective-permute-start(f32[256,256]{1,0:T(8,128)S(1)} %bitcast.30), channel_id=1, source_target_pairs={{0,5},{1,4},{8,13},{9,12},{16,21},{17,20},{24,29},{25,28},{32,37},... | collective-permute-start | bytes 786440 | tf_op jit(solution)/shard_map/ppermute | solution.py:330
  21.2 16.9 %all-to-all-start = ((f32[32,8,256]{2,1,0:T(8,128)}), f32[32,8,256]{2,1,0:T(8,128)S(1)}, u32[]{:S(2)}, u32[]{:S(2)}) async-start(f32[32,8,256]{2,1,0:T(8,128)} %bitcast.22.clone.2), calls=%async_computation | async-start | bytes 524288 | tf_op jit(solution)/shard_map/all_to_all | solution.py:331
  29.2 77.1 %all-gather.3.cloned.1.call-start = ((), (), s32[]{:S(2)}) async-start(), calls=%async_computation.3 | async-start | bytes 2359296 | tf_op jit(solution)/shard_map/all_gather | solution.py:334
  79.0 5.9 %collective-permute-start.3 = (f32[16,24,256]{2,1,0:T(8,128)S(1)}, f32[16,24,256]{2,1,0:T(8,128)S(1)}, u32[]{:S(2)}, u32[]{:S(2)}) collective-permute-start(f32[16,24,256]{2,1,0:T(8,128)S(1)} %shard_map.19.mine), channel_id=1, source_target_pairs={{0,8},{8,0},{16,24},{24,16},{32,40},{40,32},{48,56},{56,48},{64,72... | collective-permute-start | bytes 1179656 | tf_op jit(solution)/shard_map/ppermute | solution.py:340
  95.6 10.7 %collective-permute-start.4 = (f32[16,88,256]{2,1,0:T(8,128)S(1)}, f32[16,88,256]{2,1,0:T(8,128)S(1)}, u32[]{:S(2)}, u32[]{:S(2)}) collective-permute-start(f32[16,88,256]{2,1,0:T(8,128)S(1)} %get-tuple-element.19.mine), channel_id=1, source_target_pairs={{0,8},{8,0},{16,24},{24,16},{32,40},{40,32},{48,56},{56,48},{64,72... | collective-permute-start | bytes 4325384 | tf_op jit(solution)/shard_map/ppermute | solution.py:342
  105.6 0.7 copy-start
  106.3 1.0 copy-start.1
Sparse Core Ops, SparseCore 0:
  55.6 35.5 all-gather.2

commit v4 on v3

--- a/solution.py
+++ b/solution.py
@@ -68,6 +68,7 @@
 
 
 VMEM = pl.BlockSpec(memory_space=pltpu.VMEM)
+ANY = pl.BlockSpec(memory_space=pl.ANY)
 SMEM = pl.BlockSpec(memory_space=pltpu.SMEM)
 CHIPS = 16
 LEAD = 24
@@ -75,6 +76,17 @@
 
 def rows_of(chip, core):
     return pl.ds(pl.multiple_of(16 * chip + 8 * core, 8), 8)
+
+
+def small(kernel, outs, specs, *args):
+    return pl.pallas_call(
+        kernel,
+        out_shape=[jax.ShapeDtypeStruct(shape, F32) for shape in outs],
+        in_specs=specs,
+        out_specs=[VMEM] * len(outs),
+        compiler_params=pltpu.CompilerParams(vmem_limit_bytes=4 * MIB),
+        cost_estimate=pl.CostEstimate(flops=0, bytes_accessed=2 * MIB, transcendentals=0),
+    )(*args)
 
 
 def outward_kernel(where, pieces, first, got1, got2, got3, out, share):
@@ -82,17 +94,6 @@
         for i, tile in enumerate((z, z + 8, z + 16, z + 24, 0, 1)):
             out[z, 8 * i : 8 * i + 8] = pieces[tile]
     share[...] = jnp.where(where[1] < 2, first[...], got1[...] + got2[...] + got3[...])
-
-
-def outward(where, pieces, first, got):
-    return pl.pallas_call(
-        outward_kernel,
-        out_shape=[jax.ShapeDtypeStruct((8, 48, T), F32), jax.ShapeDtypeStruct((T, T), F32)],
-        in_specs=[SMEM] + [VMEM] * 5,
-        out_specs=[VMEM] * 2,
-        compiler_params=pltpu.CompilerParams(vmem_limit_bytes=4 * MIB),
-        cost_estimate=pl.CostEstimate(flops=0, bytes_accessed=MIB, transcendentals=0),
-    )(where, pieces, first, *got)
 
 
 def inward_kernel(lines, tile, out, share):
@@ -104,30 +105,12 @@
     share[...] = tile[...]
 
 
-def inward(lines, tile):
-    return pl.pallas_call(
-        inward_kernel,
-        out_shape=[jax.ShapeDtypeStruct((CHIPS, LEAD + 64, T), F32), square(T)],
-        in_specs=[VMEM] * 2,
-        out_specs=[VMEM, pl.BlockSpec((T, T), lambda: (0, 0))],
-        compiler_params=pltpu.CompilerParams(vmem_limit_bytes=4 * MIB),
-        cost_estimate=pl.CostEstimate(flops=0, bytes_accessed=2 * MIB, transcendentals=0),
-    )(lines, tile)
-
-
-def head_kernel(both, lead):
+def head_kernel(both, right, left, ready1, ready2, lead, up, down, top, bottom):
     lead[...] = both[:, 0:LEAD]
-
-
-def head(both):
-    return pl.pallas_call(
-        head_kernel,
-        out_shape=jax.ShapeDtypeStruct((CHIPS, LEAD, T), F32),
-        in_specs=[VMEM],
-        out_specs=VMEM,
-        compiler_params=pltpu.CompilerParams(vmem_limit_bytes=4 * MIB),
-        cost_estimate=pl.CostEstimate(flops=0, bytes_accessed=MIB, transcendentals=0),
-    )(both)
+    up[...] = right[...]
+    down[...] = left[...]
+    top[...] = right[0:B]
+    bottom[...] = left[B:]
 
 
 def first_kernel(where, mine, other, both, w, e_low, a_low, same, a, e, tiles):
@@ -225,13 +208,13 @@
 STEP = 256
 
 
-def update_kernel(where, a, p, mine, other, w00, w10, w11, out, buf, panel, mirror, x_out, left, right, x_cat, y_cat, sem_a, sem_p, sem_out):
+def update_kernel(where, a, *refs):
+    panels, refs = refs[:9], refs[9:]
+    mine, other, w00, w10, w11, out, buf, panel, mirror, x_out, left, right, x_cat, y_cat, sem_a, sem_out = refs
     r, c = where[0], where[1]
     core = lax.rem(r, 2)
     n_half = 4 * T * 8 // 2
     loads = [pltpu.make_async_copy(a.at[pl.ds(i * n_half, n_half)], buf.at[pl.ds(i * n_half, n_half)], sem_a.at[i]) for i in range(2)]
-    fetch = pltpu.make_async_copy(p, panel, sem_p)
-    fetch.start()
     for load in loads:
         load.start()
     for i, t in enumerate((w00, w10, w11)):
@@ -260,7 +243,10 @@
                 mirror[k, n, rows_of(j, core)] = mine[j, at : at + 8]
                 mirror[k, n, rows_of(j, 1 - core)] = other[j, at : at + 8]
     solve(mirror[0].reshape(4 * T, T), mirror[1].reshape(4 * T, T), 8, c, y_cat, (0, 0, 1), False)
-    fetch.wait()
+    for j, part in zip((0, 1, 2, 3, 5, 6, 7), panels):
+        panel[lax.rem(c - j + 8, 8)] = part[...]
+    panel[lax.rem(c + 4, 8), 0:B] = panels[7][...]
+    panel[lax.rem(c + 4, 8), B:] = panels[8][...]
     first = jnp.concatenate([panel[0], panel[7], panel[6], panel[5]], axis=0)
     solve(first, panel[1:5].reshape(4 * T, T), 32, r, x_cat, (0, 1, 0), True)
 
@@ -293,13 +279,13 @@
         store.wait()
 
 
-def update(where, a, panel, mine, other, w):
+def update(where, a, panels, mine, other, w):
     hbm = pl.BlockSpec(memory_space=pltpu.HBM)
-    a, panel = (pltpu.with_memory_space_constraint(t, pltpu.HBM) for t in (a, panel))
+    a = pltpu.with_memory_space_constraint(a, pltpu.HBM)
     return pl.pallas_call(
         update_kernel,
         out_shape=jax.ShapeDtypeStruct(a.shape, F32),
-        in_specs=[SMEM, hbm, hbm] + [VMEM] * 5,
+        in_specs=[SMEM, hbm] + [VMEM] * 14,
         out_specs=hbm,
         scratch_shapes=[
             pltpu.VMEM((4 * T * 8, B), F32),
@@ -311,12 +297,15 @@
             pltpu.VMEM((4 * T, SIX), BF16),
             pltpu.VMEM((4 * T, SIX), BF16),
             pltpu.SemaphoreType.DMA((2,)),
-            pltpu.SemaphoreType.DMA,
             pltpu.SemaphoreType.DMA((2,)),
         ],
         compiler_params=pltpu.CompilerParams(vmem_limit_bytes=38 * MIB),
         cost_estimate=pl.CostEstimate(flops=8 * 10**9, bytes_accessed=12 * MIB, transcendentals=0),
-    )(where, a, panel, mine, other, *w)
+    )(where, a, *panels, mine, other, *w)
+
+
+def along(x, step):
+    return lax.ppermute(x, "col", [(z, (z + step) % 8) for z in range(8)])
 
 
 def per_device(matrix):
@@ -326,20 +315,27 @@
     flat = matrix.reshape(4, T, 4, 2, B).transpose(0, 1, 3, 2, 4).reshape(4 * T * 8, B)
     column = matrix[:, :, 0, :]
     first = column[0]
+    tile = (T, T)
+    half = (B, T)
 
     got = [lax.ppermute(column[m], "col", [(0, 8 - m), (1, 1 + m)]) for m in (1, 2, 3)]
     pieces = lax.all_to_all(first.reshape(32, 8, T), "row", 0, 0)
-    spread, tile = outward(where, pieces, first, got)
-    both, share = inward(lax.all_to_all(spread, "col", 0, 0), tile)
-    panel = lax.all_gather(share, "col", axis=0)
+    spread, share = small(outward_kernel, [(8, 48, T), tile], [SMEM] + [VMEM] * 5, where, pieces, first, *got)
+    lines = lax.all_to_all(spread, "col", 0, 0)
+    both, share = small(inward_kernel, [(CHIPS, LEAD + 64, T), tile], [VMEM] * 2, lines, share)
+    near = [along(share, step) for step in (1, 2, -2, -1)]
 
     cores = [[2 * j + k for j in range(CHIPS)] for k in range(2)]
     swap = [(i, i ^ 1) for i in range(32)]
     both = lax.all_to_all(both, "row", 0, 0, axis_index_groups=cores)
-    lead = head(both)
+    lead, up, down, top, bottom = small(
+        head_kernel, [(CHIPS, LEAD, T), tile, tile, half, half], [VMEM] * 3 + [ANY] * 2, both, near[1], near[2], near[0], near[3]
+    )
+    far = [along(up, 1), along(down, -1), along(top, 2), along(bottom, -2)]
     w00, e_low, a_low, both = first_factor(where, lead, lax.ppermute(lead, "row", swap), both)
     w11, w10 = second_factor(a_low, e_low)
-    out = update(where, flat, panel, both, lax.ppermute(both, "row", swap), (w00, w10, w11))
+    panels = [share, near[0], near[1], far[0], far[1], near[2], near[3], far[2], far[3]]
+    out = update(where, flat, panels, both, lax.ppermute(both, "row", swap), (w00, w10, w11))
     return out.reshape(4, T, 2, 4, B).transpose(0, 1, 3, 2, 4).reshape(4, T, 4, T)
 
 

time: 129 us -> 122 us (0.946)
  blocking collectives: 38.9 us -> 15.4 us
  waiting for transfers between devices: 10.1 us -> 30 us
  between operations: 13.5 us -> 0.36 us
  starting transfers between devices: 24.2 us -> 36.5 us
  local copies, waits for them, and re-layouts: 5.33 us -> 3.67 us
    all_to_all x2 -> x1, blocking collectives: 38.9 us -> 15.4 us  [per_device(): lines = lax.all_to_all(spread, 'col', 0, 0)]
    ppermute x0 -> x8, waiting for transfers between devices: none -> 19.8 us  [along(): return lax.ppermute(x, 'col', [(z, (z + step) % 8) for z in range(8)])]
    ppermute x0 -> x8, starting transfers between devices: none -> 10.2 us  [along(): return lax.ppermute(x, 'col', [(z, (z + step) % 8) for z in range(8)])]
    all_to_all x0 -> x1, starting transfers between devices: none -> 5.75 us  [per_device(): both = lax.all_to_all(both, 'row', 0, 0, axis_index_groups=cores)]
    ppermute x1, starting transfers between devices: 4.56 us -> 1.18 us  [per_device(): lax.ppermute(lead, 'row', swap)]
    unnamed x8 -> x4, local copies, waits for them, and re-layouts: 2.44 us -> 0.78 us
    pallas_call x1, Pallas kernels: 14.2 us -> 12.8 us  [update(): pl.pallas_call(update_kernel, out_shape=jax.ShapeDtypeStruct(a.shape, F32...]
  transfers between devices with their start and end apart: 7 -> 15, of which waited for: 2 -> 5; matrix products, arithmetic and copies ran while one was open for 1% -> 1% of each run, Pallas kernels for 16% -> 8%
where the time goes in v4:
time: 122 us; the launch traced here: 121 us
  starting transfers between devices  36.5 us (30%)
  Pallas kernels  35.2 us (29%)
  waiting for transfers between devices  30 us (25%)
  blocking collectives  15.4 us (13%)
  local copies, waits for them, and re-layouts  3.67 us (3%)
    ppermute x8, waiting for transfers between devices, along(): return lax.ppermute(x, 'col', [(z, (z + step) % 8) for z in range(8)])  19.8 us
    all_to_all x1, blocking collectives, per_device(): lines = lax.all_to_all(spread, 'col', 0, 0)  15.4 us
    pallas_call x1, Pallas kernels, update(): pl.pallas_call(update_kernel, out_shape=jax.ShapeDtypeStruct(a.shape, F32...  12.8 us
    ppermute x3, starting transfers between devices, per_device(): lax.ppermute(column[m], 'col', [(0, 8 - m), (1, 1 + m)])  10.9 us
    pallas_call x1, Pallas kernels, first_factor(): pl.pallas_call(first_kernel, out_shape=[square(T)] * 3 + [jax.ShapeDtypeS...  10.7 us
    ppermute x8, starting transfers between devices, along(): return lax.ppermute(x, 'col', [(z, (z + step) % 8) for z in range(8)])  10.2 us
    pallas_call x1, Pallas kernels, second_factor(): pl.pallas_call(second_kernel, out_shape=[square(T)] * 2, in_specs=[VMEM]...  9.36 us
    all_to_all x1, waiting for transfers between devices, per_device(): pieces = lax.all_to_all(first.reshape(32, 8, T), 'row', 0, 0)  8.82 us
  transfers between devices with their start and end apart: 15, of which 5 were waited for; matrix products, arithmetic and copies ran while one was open for 1% of the time, Pallas kernels for 8%

profile of v4, /device:TPU:1, one launch (start us, length us, event | category | flops | bytes accessed | tf_op | source)
XLA Modules:
  0.0 121.2 jit_solution(14869751886529308907)
XLA Ops:
  0.0 2.9 %fusion = (f32[1,256,1,256]{3,2,1,0:T(1,128)S(1)}, f32[1,256,1,256]{3,2,1,0:T(1,128)S(1)}, f32[1,256,1,256]{3,2,1,0:T(1,128)S(1)}, f32[1,256,1,256]{3,2,1,0:T(1,128)S(1)}) fusion(f32[4,256,4,256]{3,2,1,0:T(4,128)} %param.1), kind=kLoop, calls=%fused_computation.6 | loop fusion | bytes 2097152 | tf_op jit(solution)/shard_map/slice | solution.py:321
  2.9 8.3 %collective-permute-start = (f32[256,256]{1,0:T(8,128)S(1)}, f32[256,256]{1,0:T(8,128)S(1)}, u32[]{:S(2)}, u32[]{:S(2)}) collective-permute-start(f32[256,256]{1,0:T(8,128)S(1)} %bitcast.27), channel_id=1, source_target_pairs={{0,7},{1,2},{8,15},{9,10},{16,23},{17,18},{24,31},{25,26},{32,39},... | collective-permute-start | bytes 786440 | tf_op jit(solution)/shard_map/ppermute | solution.py:321
  11.3 1.3 %collective-permute-start.1 = (f32[256,256]{1,0:T(8,128)S(1)}, f32[256,256]{1,0:T(8,128)S(1)}, u32[]{:S(2)}, u32[]{:S(2)}) collective-permute-start(f32[256,256]{1,0:T(8,128)S(1)} %bitcast.28), channel_id=1, source_target_pairs={{0,6},{1,3},{8,14},{9,11},{16,22},{17,19},{24,30},{25,27},{32,38},... | collective-permute-start | bytes 786440 | tf_op jit(solution)/shard_map/ppermute | solution.py:321
  12.6 1.3 %collective-permute-start.2 = (f32[256,256]{1,0:T(8,128)S(1)}, f32[256,256]{1,0:T(8,128)S(1)}, u32[]{:S(2)}, u32[]{:S(2)}) collective-permute-start(f32[256,256]{1,0:T(8,128)S(1)} %bitcast.29), channel_id=1, source_target_pairs={{0,5},{1,4},{8,13},{9,12},{16,21},{17,20},{24,29},{25,28},{32,37},... | collective-permute-start | bytes 786440 | tf_op jit(solution)/shard_map/ppermute | solution.py:321
  13.9 0.7 copy.21
  14.7 8.0 %all-to-all-start = ((f32[32,8,256]{2,1,0:T(8,128)}), f32[32,8,256]{2,1,0:T(8,128)S(1)}, u32[]{:S(2)}, u32[]{:S(2)}) async-start(f32[32,8,256]{2,1,0:T(8,128)} %bitcast.21.clone.2), calls=%async_computation | async-start | bytes 524288 | tf_op jit(solution)/shard_map/all_to_all | solution.py:322
  22.8 8.8 %all-to-all-done.pieces = f32[32,8,256]{2,1,0:T(8,128)S(1)} async-done(((f32[32,8,256]{2,1,0:T(8,128)}), f32[32,8,256]{2,1,0:T(8,128)S(1)}, u32[]{:S(2)}, u32[]{:S(2)}) %all-to-all-start) | async-done | bytes 262176 | tf_op jit(solution)/shard_map/all_to_all | solution.py:322
  31.6 1.0 shard_map.17
  32.7 15.4 %all_to_all.15.lines = f32[8,48,256]{2,1,0:T(8,128)S(1)} all-to-all(f32[8,48,256]{2,1,0:T(8,128)S(1)} %get-tuple-element.20), channel_id=1, replica_groups=mesh['row'=32,'col'=8] {'col'}, dimensions={0} | all-to-all | bytes 786432 | tf_op jit(solution)/shard_map/all_to_all | solution.py:324
  48.1 1.2 shard_map.18
  49.3 5.8 %all-to-all-start.2 = ((f32[16,88,256]{2,1,0:T(8,128)}), f32[16,88,256]{2,1,0:T(8,128)S(1)}, u32[]{:S(2)}, u32[]{:S(2)}) async-start(f32[16,88,256]{2,1,0:T(8,128)} %get-tuple-element.23), calls=%async_computation.2 | async-start | bytes 2883584 | tf_op jit(solution)/shard_map/all_to_all | solution.py:330
  55.1 2.3 %collective-permute-start.5 = (f32[256,256]{1,0:T(8,128)S(1)}, f32[256,256]{1,0:T(8,128)S(1)}, u32[]{:S(2)}, u32[]{:S(2)}) collective-permute-start(f32[256,256]{1,0:T(8,128)S(1)} %get-tuple-element.22.refs_0_), channel_id=1, source_target_pairs={{0,6},{1,7},{2,0},{3,1},{4,2},{5,3},{6,4},{7,5},{8,14},{9,15},{10,... | collective-permute-start | bytes 786440 | tf_op jit(solution)/shard_map/ppermute | solution.py:308
  57.6 1.4 %collective-permute-start.3 = (f32[256,256]{1,0:T(8,128)S(1)}, f32[256,256]{1,0:T(8,128)S(1)}, u32[]{:S(2)}, u32[]{:S(2)}) collective-permute-start(f32[256,256]{1,0:T(8,128)S(1)} %get-tuple-element.22.refs_0_), channel_id=1, source_target_pairs={{0,1},{1,2},{2,3},{3,4},{4,5},{5,6},{6,7},{7,0},{8,9},{9,10},{10,1... | collective-permute-start | bytes 786440 | tf_op jit(solution)/shard_map/ppermute | solution.py:308
  59.0 2.2 %collective-permute-done.6.ready2.refs_6_ = f32[256,256]{1,0:T(8,128)S(1)} collective-permute-done((f32[256,256]{1,0:T(8,128)S(1)}, f32[256,256]{1,0:T(8,128)S(1)}, u32[]{:S(2)}, u32[]{:S(2)}) %collective-permute-start.6) | collective-permute-done | bytes 262176 | tf_op jit(solution)/shard_map/ppermute | solution.py:308
  61.2 7.9 %collective-permute-done.5.left.refs_5_ = f32[256,256]{1,0:T(8,128)S(1)} collective-permute-done((f32[256,256]{1,0:T(8,128)S(1)}, f32[256,256]{1,0:T(8,128)S(1)}, u32[]{:S(2)}, u32[]{:S(2)}) %collective-permute-start.5) | collective-permute-done | bytes 262176 | tf_op jit(solution)/shard_map/ppermute | solution.py:308
  69.1 9.7 %collective-permute-done.3.ready1.refs_1_ = f32[256,256]{1,0:T(8,128)S(1)} collective-permute-done((f32[256,256]{1,0:T(8,128)S(1)}, f32[256,256]{1,0:T(8,128)S(1)}, u32[]{:S(2)}, u32[]{:S(2)}) %collective-permute-start.3) | collective-permute-done | bytes 262176 | tf_op jit(solution)/shard_map/ppermute | solution.py:308
  78.8 1.2 collective-permute-start.11
  80.0 1.3 %collective-permute-done.11.other = f32[16,24,256]{2,1,0:T(8,128)S(1)} collective-permute-done((f32[16,24,256]{2,1,0:T(8,128)S(1)}, f32[16,24,256]{2,1,0:T(8,128)S(1)}, u32[]{:S(2)}, u32[]{:S(2)}) %collective-permute-start.11) | collective-permute-done | bytes 393248 | tf_op jit(solution)/shard_map/ppermute | solution.py:335
  81.4 10.7 %shard_map.20 = (f32[256,256]{1,0:T(8,128)S(1)}, f32[256,256]{1,0:T(8,128)S(1)}, f32[256,256]{1,0:T(8,128)S(1)}, f32[16,88,256]{2,1,0:T(8,128)S(1)}) custom-call(s32[2]{0:T(128)S(1)} %pad_add_fusion.where, f32[16,24,256]{2,1,0:T(8,128)S(1)} %get-tuple-element.28.mine, ...), custom_call_target="tpu_custom_call", output_to_operand_aliasing={{3}: (3, {})} | custom-call | flops 1000000000 | bytes 41943040 | tf_op jit(solution)/shard_map/pallas_call | solution.py:160
  92.1 0.5 collective-permute-start.12
  92.5 2.7 %collective-permute-start.8 = (f32[256,256]{1,0:T(8,128)S(1)}, f32[256,256]{1,0:T(8,128)S(1)}, u32[]{:S(2)}, u32[]{:S(2)}) collective-permute-start(f32[256,256]{1,0:T(8,128)S(1)} %get-tuple-element.25), channel_id=1, source_target_pairs={{0,7},{1,0},{2,1},{3,2},{4,3},{5,4},{6,5},{7,6},{8,15},{9,8},{10,9... | collective-permute-start | bytes 786440 | tf_op jit(solution)/shard_map/ppermute | solution.py:308
  95.2 3.6 %collective-permute-start.10 = (f32[128,256]{1,0:T(8,128)S(1)}, f32[128,256]{1,0:T(8,128)S(1)}, u32[]{:S(2)}, u32[]{:S(2)}) collective-permute-start(f32[128,256]{1,0:T(8,128)S(1)} %get-tuple-element.27), channel_id=1, source_target_pairs={{0,6},{1,7},{2,0},{3,1},{4,2},{5,3},{6,4},{7,5},{8,14},{9,15},{10,... | collective-permute-start | bytes 393224 | tf_op jit(solution)/shard_map/ppermute | solution.py:308
  98.8 9.4 %shard_map.21 = (f32[256,256]{1,0:T(8,128)S(1)}, f32[256,256]{1,0:T(8,128)S(1)}) custom-call(f32[256,256]{1,0:T(8,128)S(1)} %get-tuple-element.31.a, f32[256,256]{1,0:T(8,128)S(1)} %get-tuple-element.32.e_low), custom_call_target="tpu_custom_call" | custom-call | flops 1000000000 | bytes 41943040 | tf_op jit(solution)/shard_map/pallas_call | solution.py:173
  108.2 12.8 %shard_map.22 = f32[8192,128]{1,0:T(8,128)} custom-call(s32[2]{0:T(128)S(1)} %pad_add_fusion.where, f32[8192,128]{1,0:T(8,128)} %bitcast.26, f32[256,256]{1,0:T(8,128)S(1)} %get-tuple-element.22.refs_0_, f32[256,256]{1,0:T(8,128)S(1)} %collective-permute-done.3.ready1.refs_1_, f32[256,256]{1,0:T(8,128)S(1)} %collective-permute-done.4.right.refs_2_, ...), custom_call_target="tpu_custom_call" | custom-call | flops 8000000000 | bytes 12582912 | tf_op jit(solution)/shard_map/pallas_call | solution.py:285
  (19 shorter events, 0.5 us)
Async XLA Ops:
  2.9 28.7 %collective-permute-start = (f32[256,256]{1,0:T(8,128)S(1)}, f32[256,256]{1,0:T(8,128)S(1)}, u32[]{:S(2)}, u32[]{:S(2)}) collective-permute-start(f32[256,256]{1,0:T(8,128)S(1)} %bitcast.27), channel_id=1, source_target_pairs={{0,7},{1,2},{8,15},{9,10},{16,23},{17,18},{24,31},{25,26},{32,39},... | collective-permute-start | bytes 786440 | tf_op jit(solution)/shard_map/ppermute | solution.py:321
  11.3 20.3 %collective-permute-start.1 = (f32[256,256]{1,0:T(8,128)S(1)}, f32[256,256]{1,0:T(8,128)S(1)}, u32[]{:S(2)}, u32[]{:S(2)}) collective-permute-start(f32[256,256]{1,0:T(8,128)S(1)} %bitcast.28), channel_id=1, source_target_pairs={{0,6},{1,3},{8,14},{9,11},{16,22},{17,19},{24,30},{25,27},{32,38},... | collective-permute-start | bytes 786440 | tf_op jit(solution)/shard_map/ppermute | solution.py:321
  12.6 19.0 %collective-permute-start.2 = (f32[256,256]{1,0:T(8,128)S(1)}, f32[256,256]{1,0:T(8,128)S(1)}, u32[]{:S(2)}, u32[]{:S(2)}) collective-permute-start(f32[256,256]{1,0:T(8,128)S(1)} %bitcast.29), channel_id=1, source_target_pairs={{0,5},{1,4},{8,13},{9,12},{16,21},{17,20},{24,29},{25,28},{32,37},... | collective-permute-start | bytes 786440 | tf_op jit(solution)/shard_map/ppermute | solution.py:321
  14.7 16.9 %all-to-all-start = ((f32[32,8,256]{2,1,0:T(8,128)}), f32[32,8,256]{2,1,0:T(8,128)S(1)}, u32[]{:S(2)}, u32[]{:S(2)}) async-start(f32[32,8,256]{2,1,0:T(8,128)} %bitcast.21.clone.2), calls=%async_computation | async-start | bytes 524288 | tf_op jit(solution)/shard_map/all_to_all | solution.py:322
  49.3 29.5 %all-to-all-start.2 = ((f32[16,88,256]{2,1,0:T(8,128)}), f32[16,88,256]{2,1,0:T(8,128)S(1)}, u32[]{:S(2)}, u32[]{:S(2)}) async-start(f32[16,88,256]{2,1,0:T(8,128)} %get-tuple-element.23), calls=%async_computation.2 | async-start | bytes 2883584 | tf_op jit(solution)/shard_map/all_to_all | solution.py:330
  55.1 6.1 %collective-permute-start.6 = (f32[256,256]{1,0:T(8,128)S(1)}, f32[256,256]{1,0:T(8,128)S(1)}, u32[]{:S(2)}, u32[]{:S(2)}) collective-permute-start(f32[256,256]{1,0:T(8,128)S(1)} %get-tuple-element.22.refs_0_), channel_id=1, source_target_pairs={{0,7},{1,0},{2,1},{3,2},{4,3},{5,4},{6,5},{7,6},{8,15},{9,8},{10,9... | collective-permute-start | bytes 786440 | tf_op jit(solution)/shard_map/ppermute | solution.py:308
  55.1 13.9 %collective-permute-start.5 = (f32[256,256]{1,0:T(8,128)S(1)}, f32[256,256]{1,0:T(8,128)S(1)}, u32[]{:S(2)}, u32[]{:S(2)}) collective-permute-start(f32[256,256]{1,0:T(8,128)S(1)} %get-tuple-element.22.refs_0_), channel_id=1, source_target_pairs={{0,6},{1,7},{2,0},{3,1},{4,2},{5,3},{6,4},{7,5},{8,14},{9,15},{10,... | collective-permute-start | bytes 786440 | tf_op jit(solution)/shard_map/ppermute | solution.py:308
  57.4 11.7 %collective-permute-start.4 = (f32[256,256]{1,0:T(8,128)S(1)}, f32[256,256]{1,0:T(8,128)S(1)}, u32[]{:S(2)}, u32[]{:S(2)}) collective-permute-start(f32[256,256]{1,0:T(8,128)S(1)} %get-tuple-element.22.refs_0_), channel_id=1, source_target_pairs={{0,2},{1,3},{2,4},{3,5},{4,6},{5,7},{6,0},{7,1},{8,10},{9,11},{10,... | collective-permute-start | bytes 786440 | tf_op jit(solution)/shard_map/ppermute | solution.py:308
  57.6 21.2 %collective-permute-start.3 = (f32[256,256]{1,0:T(8,128)S(1)}, f32[256,256]{1,0:T(8,128)S(1)}, u32[]{:S(2)}, u32[]{:S(2)}) collective-permute-start(f32[256,256]{1,0:T(8,128)S(1)} %get-tuple-element.22.refs_0_), channel_id=1, source_target_pairs={{0,1},{1,2},{2,3},{3,4},{4,5},{5,6},{6,7},{7,0},{8,9},{9,10},{10,1... | collective-permute-start | bytes 786440 | tf_op jit(solution)/shard_map/ppermute | solution.py:308
  78.8 2.5 %collective-permute-start.11 = (f32[16,24,256]{2,1,0:T(8,128)S(1)}, f32[16,24,256]{2,1,0:T(8,128)S(1)}, u32[]{:S(2)}, u32[]{:S(2)}) collective-permute-start(f32[16,24,256]{2,1,0:T(8,128)S(1)} %get-tuple-element.28.mine), channel_id=1, source_target_pairs={{0,8},{8,0},{16,24},{24,16},{32,40},{40,32},{48,56},{56,48},{64,72... | collective-permute-start | bytes 1179656 | tf_op jit(solution)/shard_map/ppermute | solution.py:335
  92.1 16.1 %collective-permute-start.12 = (f32[16,88,256]{2,1,0:T(8,128)S(1)}, f32[16,88,256]{2,1,0:T(8,128)S(1)}, u32[]{:S(2)}, u32[]{:S(2)}) collective-permute-start(f32[16,88,256]{2,1,0:T(8,128)S(1)} %get-tuple-element.29.refs_9_), channel_id=1, source_target_pairs={{0,8},{8,0},{16,24},{24,16},{32,40},{40,32},{48,56},{56,48},{64,72... | collective-permute-start | bytes 4325384 | tf_op jit(solution)/shard_map/ppermute | solution.py:338
  92.5 15.6 %collective-permute-start.7 = (f32[256,256]{1,0:T(8,128)S(1)}, f32[256,256]{1,0:T(8,128)S(1)}, u32[]{:S(2)}, u32[]{:S(2)}) collective-permute-start(f32[256,256]{1,0:T(8,128)S(1)} %get-tuple-element.24), channel_id=1, source_target_pairs={{0,1},{1,2},{2,3},{3,4},{4,5},{5,6},{6,7},{7,0},{8,9},{9,10},{10,1... | collective-permute-start | bytes 786440 | tf_op jit(solution)/shard_map/ppermute | solution.py:308
  92.5 15.7 %collective-permute-start.8 = (f32[256,256]{1,0:T(8,128)S(1)}, f32[256,256]{1,0:T(8,128)S(1)}, u32[]{:S(2)}, u32[]{:S(2)}) collective-permute-start(f32[256,256]{1,0:T(8,128)S(1)} %get-tuple-element.25), channel_id=1, source_target_pairs={{0,7},{1,0},{2,1},{3,2},{4,3},{5,4},{6,5},{7,6},{8,15},{9,8},{10,9... | collective-permute-start | bytes 786440 | tf_op jit(solution)/shard_map/ppermute | solution.py:308
  95.2 12.9 %collective-permute-start.9 = (f32[128,256]{1,0:T(8,128)S(1)}, f32[128,256]{1,0:T(8,128)S(1)}, u32[]{:S(2)}, u32[]{:S(2)}) collective-permute-start(f32[128,256]{1,0:T(8,128)S(1)} %get-tuple-element.26), channel_id=1, source_target_pairs={{0,2},{1,3},{2,4},{3,5},{4,6},{5,7},{6,0},{7,1},{8,10},{9,11},{10,... | collective-permute-start | bytes 393224 | tf_op jit(solution)/shard_map/ppermute | solution.py:308
  95.2 13.0 %collective-permute-start.10 = (f32[128,256]{1,0:T(8,128)S(1)}, f32[128,256]{1,0:T(8,128)S(1)}, u32[]{:S(2)}, u32[]{:S(2)}) collective-permute-start(f32[128,256]{1,0:T(8,128)S(1)} %get-tuple-element.27), channel_id=1, source_target_pairs={{0,6},{1,7},{2,0},{3,1},{4,2},{5,3},{6,4},{7,5},{8,14},{9,15},{10,... | collective-permute-start | bytes 393224 | tf_op jit(solution)/shard_map/ppermute | solution.py:308

commit v5 on v4

--- a/solution.py
+++ b/solution.py
@@ -89,6 +89,30 @@
     )(*args)
 
 
+def column_kernel(a, *refs):
+    outs, (buf, sem) = refs[:4], refs[4:]
+    size = 8 * T
+    loads = [pltpu.make_async_copy(a.at[pl.ds(m * size, size)], buf.at[pl.ds(m * size, size)], sem.at[m]) for m in range(4)]
+    for load in loads:
+        load.start()
+    for m in range(4):
+        loads[m].wait()
+        for half in range(2):
+            outs[m][:, half * B : (half + 1) * B] = buf[pl.ds(m * size + half * 4, T, stride=8), :]
+
+
+def tile_column(a):
+    return pl.pallas_call(
+        column_kernel,
+        out_shape=[square(T)] * 4,
+        in_specs=[pl.BlockSpec(memory_space=pltpu.HBM)],
+        out_specs=[VMEM] * 4,
+        scratch_shapes=[pltpu.VMEM((4 * T * 8, B), F32), pltpu.SemaphoreType.DMA((4,))],
+        compiler_params=pltpu.CompilerParams(vmem_limit_bytes=8 * MIB),
+        cost_estimate=pl.CostEstimate(flops=0, bytes_accessed=5 * MIB, transcendentals=0),
+    )(pltpu.with_memory_space_constraint(a, pltpu.HBM))
+
+
 def outward_kernel(where, pieces, first, got1, got2, got3, out, share):
     for z in range(8):
         for i, tile in enumerate((z, z + 8, z + 16, z + 24, 0, 1)):
@@ -313,7 +337,7 @@
     c = lax.axis_index("col")
     where = jnp.stack([r, c]).astype(jnp.int32)
     flat = matrix.reshape(4, T, 4, 2, B).transpose(0, 1, 3, 2, 4).reshape(4 * T * 8, B)
-    column = matrix[:, :, 0, :]
+    column = tile_column(flat)
     first = column[0]
     tile = (T, T)
     half = (B, T)

time: 122 us -> 122 us (level)
  local copies, waits for them, and re-layouts: 3.67 us -> 0 us
  Pallas kernels: 35.2 us -> 38.1 us
    pallas_call x0 -> x1, Pallas kernels: none -> 2.91 us  [tile_column(): pl.pallas_call(column_kernel, out_shape=[square(T)] * 4, in_specs=[pl.Blo...]
    slice x1 -> x0, local copies, waits for them, and re-layouts: 2.89 us -> none  [per_device(): column[m]]
  transfers between devices with their start and end apart: 15 -> 15, of which waited for: 5 -> 5; matrix products, arithmetic and copies ran while one was open for 1% -> 0% of each run, Pallas kernels for 8% -> 8%
where the time goes in v5:
time: 122 us; the launch traced here: 121 us
  Pallas kernels  38.1 us (31%)
  starting transfers between devices  37.5 us (31%)
  waiting for transfers between devices  30 us (25%)
  blocking collectives  15.2 us (12%)
    ppermute x8, waiting for transfers between devices, along(): return lax.ppermute(x, 'col', [(z, (z + step) % 8) for z in range(8)])  19.8 us
    all_to_all x1, blocking collectives, per_device(): lines = lax.all_to_all(spread, 'col', 0, 0)  15.2 us
    pallas_call x1, Pallas kernels, update(): pl.pallas_call(update_kernel, out_shape=jax.ShapeDtypeStruct(a.shape, F32...  12.8 us
    ppermute x3, starting transfers between devices, per_device(): lax.ppermute(column[m], 'col', [(0, 8 - m), (1, 1 + m)])  10.9 us
    pallas_call x1, Pallas kernels, first_factor(): pl.pallas_call(first_kernel, out_shape=[square(T)] * 3 + [jax.ShapeDtypeS...  10.7 us
    ppermute x8, starting transfers between devices, along(): return lax.ppermute(x, 'col', [(z, (z + step) % 8) for z in range(8)])  10.2 us
    pallas_call x1, Pallas kernels, second_factor(): pl.pallas_call(second_kernel, out_shape=[square(T)] * 2, in_specs=[VMEM]...  9.36 us
    all_to_all x1, waiting for transfers between devices, per_device(): pieces = lax.all_to_all(first.reshape(32, 8, T), 'row', 0, 0)  8.82 us
  transfers between devices with their start and end apart: 15, of which 5 were waited for; matrix products, arithmetic and copies ran while one was open for 0% of the time, Pallas kernels for 8%

profile of v5, /device:TPU:1, one launch (start us, length us, event | category | flops | bytes accessed | tf_op | source)
XLA Modules:
  0.0 121.2 jit_solution(3527233077472364139)
XLA Ops:
  0.0 2.9 %shard_map.17 = (f32[256,256]{1,0:T(8,128)}, f32[256,256]{1,0:T(8,128)S(1)}, f32[256,256]{1,0:T(8,128)S(1)}, f32[256,256]{1,0:T(8,128)S(1)}) custom-call(f32[8192,128]{1,0:T(8,128)} %bitcast.13), custom_call_target="tpu_custom_call" | custom-call | bytes 5242880 | tf_op jit(solution)/shard_map/pallas_call | solution.py:105
  2.9 8.3 %collective-permute-start = (f32[256,256]{1,0:T(8,128)S(1)}, f32[256,256]{1,0:T(8,128)S(1)}, u32[]{:S(2)}, u32[]{:S(2)}) collective-permute-start(f32[256,256]{1,0:T(8,128)S(1)} %get-tuple-element.25), channel_id=1, source_target_pairs={{0,7},{1,2},{8,15},{9,10},{16,23},{17,18},{24,31},{25,26},{32,39},... | collective-permute-start | bytes 786440 | tf_op jit(solution)/shard_map/ppermute | solution.py:345
  11.2 1.3 %collective-permute-start.1 = (f32[256,256]{1,0:T(8,128)S(1)}, f32[256,256]{1,0:T(8,128)S(1)}, u32[]{:S(2)}, u32[]{:S(2)}) collective-permute-start(f32[256,256]{1,0:T(8,128)S(1)} %get-tuple-element.26), channel_id=1, source_target_pairs={{0,6},{1,3},{8,14},{9,11},{16,22},{17,19},{24,30},{25,27},{32,38},... | collective-permute-start | bytes 786440 | tf_op jit(solution)/shard_map/ppermute | solution.py:345
  12.6 1.3 %collective-permute-start.2 = (f32[256,256]{1,0:T(8,128)S(1)}, f32[256,256]{1,0:T(8,128)S(1)}, u32[]{:S(2)}, u32[]{:S(2)}) collective-permute-start(f32[256,256]{1,0:T(8,128)S(1)} %get-tuple-element.27), channel_id=1, source_target_pairs={{0,5},{1,4},{8,13},{9,12},{16,21},{17,20},{24,29},{25,28},{32,37},... | collective-permute-start | bytes 786440 | tf_op jit(solution)/shard_map/ppermute | solution.py:345
  13.9 8.1 %all-to-all-start = ((f32[32,8,256]{2,1,0:T(8,128)}), f32[32,8,256]{2,1,0:T(8,128)S(1)}, u32[]{:S(2)}, u32[]{:S(2)}) async-start(f32[32,8,256]{2,1,0:T(8,128)} %bitcast.7), calls=%async_computation | async-start | bytes 524288 | tf_op jit(solution)/shard_map/all_to_all | solution.py:346
  22.0 8.8 %all-to-all-done.pieces = f32[32,8,256]{2,1,0:T(8,128)S(1)} async-done(((f32[32,8,256]{2,1,0:T(8,128)}), f32[32,8,256]{2,1,0:T(8,128)S(1)}, u32[]{:S(2)}, u32[]{:S(2)}) %all-to-all-start) | async-done | bytes 262176 | tf_op jit(solution)/shard_map/all_to_all | solution.py:346
  30.8 1.0 shard_map.18
  31.9 15.2 %all_to_all.15.lines = f32[8,48,256]{2,1,0:T(8,128)S(1)} all-to-all(f32[8,48,256]{2,1,0:T(8,128)S(1)} %get-tuple-element.28), channel_id=1, replica_groups=mesh['row'=32,'col'=8] {'col'}, dimensions={0} | all-to-all | bytes 786432 | tf_op jit(solution)/shard_map/all_to_all | solution.py:348
  47.1 1.2 shard_map.19
  48.3 6.8 %all-to-all-start.2 = ((f32[16,88,256]{2,1,0:T(8,128)}), f32[16,88,256]{2,1,0:T(8,128)S(1)}, u32[]{:S(2)}, u32[]{:S(2)}) async-start(f32[16,88,256]{2,1,0:T(8,128)} %get-tuple-element.31), calls=%async_computation.2 | async-start | bytes 2883584 | tf_op jit(solution)/shard_map/all_to_all | solution.py:354
  55.1 2.3 %collective-permute-start.5 = (f32[256,256]{1,0:T(8,128)S(1)}, f32[256,256]{1,0:T(8,128)S(1)}, u32[]{:S(2)}, u32[]{:S(2)}) collective-permute-start(f32[256,256]{1,0:T(8,128)S(1)} %get-tuple-element.30.refs_0_), channel_id=1, source_target_pairs={{0,6},{1,7},{2,0},{3,1},{4,2},{5,3},{6,4},{7,5},{8,14},{9,15},{10,... | collective-permute-start | bytes 786440 | tf_op jit(solution)/shard_map/ppermute | solution.py:332
  57.4 0.2 collective-permute-start.4
  57.6 1.4 %collective-permute-start.3 = (f32[256,256]{1,0:T(8,128)S(1)}, f32[256,256]{1,0:T(8,128)S(1)}, u32[]{:S(2)}, u32[]{:S(2)}) collective-permute-start(f32[256,256]{1,0:T(8,128)S(1)} %get-tuple-element.30.refs_0_), channel_id=1, source_target_pairs={{0,1},{1,2},{2,3},{3,4},{4,5},{5,6},{6,7},{7,0},{8,9},{9,10},{10,1... | collective-permute-start | bytes 786440 | tf_op jit(solution)/shard_map/ppermute | solution.py:332
  59.0 2.2 %collective-permute-done.6.ready2.refs_6_ = f32[256,256]{1,0:T(8,128)S(1)} collective-permute-done((f32[256,256]{1,0:T(8,128)S(1)}, f32[256,256]{1,0:T(8,128)S(1)}, u32[]{:S(2)}, u32[]{:S(2)}) %collective-permute-start.6) | collective-permute-done | bytes 262176 | tf_op jit(solution)/shard_map/ppermute | solution.py:332
  61.1 7.9 %collective-permute-done.5.left.refs_5_ = f32[256,256]{1,0:T(8,128)S(1)} collective-permute-done((f32[256,256]{1,0:T(8,128)S(1)}, f32[256,256]{1,0:T(8,128)S(1)}, u32[]{:S(2)}, u32[]{:S(2)}) %collective-permute-start.5) | collective-permute-done | bytes 262176 | tf_op jit(solution)/shard_map/ppermute | solution.py:332
  69.1 9.7 %collective-permute-done.3.ready1.refs_1_ = f32[256,256]{1,0:T(8,128)S(1)} collective-permute-done((f32[256,256]{1,0:T(8,128)S(1)}, f32[256,256]{1,0:T(8,128)S(1)}, u32[]{:S(2)}, u32[]{:S(2)}) %collective-permute-start.3) | collective-permute-done | bytes 262176 | tf_op jit(solution)/shard_map/ppermute | solution.py:332
  78.8 1.2 collective-permute-start.11
  80.0 1.3 %collective-permute-done.11.other = f32[16,24,256]{2,1,0:T(8,128)S(1)} collective-permute-done((f32[16,24,256]{2,1,0:T(8,128)S(1)}, f32[16,24,256]{2,1,0:T(8,128)S(1)}, u32[]{:S(2)}, u32[]{:S(2)}) %collective-permute-start.11) | collective-permute-done | bytes 393248 | tf_op jit(solution)/shard_map/ppermute | solution.py:359
  81.4 10.7 %shard_map.21 = (f32[256,256]{1,0:T(8,128)S(1)}, f32[256,256]{1,0:T(8,128)S(1)}, f32[256,256]{1,0:T(8,128)S(1)}, f32[16,88,256]{2,1,0:T(8,128)S(1)}) custom-call(s32[2]{0:T(128)S(1)} %pad_add_fusion.where, f32[16,24,256]{2,1,0:T(8,128)S(1)} %get-tuple-element.36.mine, ...), custom_call_target="tpu_custom_call", output_to_operand_aliasing={{3}: (3, {})} | custom-call | flops 1000000000 | bytes 41943040 | tf_op jit(solution)/shard_map/pallas_call | solution.py:184
  92.1 0.5 collective-permute-start.12
  92.5 2.7 %collective-permute-start.8 = (f32[256,256]{1,0:T(8,128)S(1)}, f32[256,256]{1,0:T(8,128)S(1)}, u32[]{:S(2)}, u32[]{:S(2)}) collective-permute-start(f32[256,256]{1,0:T(8,128)S(1)} %get-tuple-element.33), channel_id=1, source_target_pairs={{0,7},{1,0},{2,1},{3,2},{4,3},{5,4},{6,5},{7,6},{8,15},{9,8},{10,9... | collective-permute-start | bytes 786440 | tf_op jit(solution)/shard_map/ppermute | solution.py:332
  95.2 3.6 %collective-permute-start.10 = (f32[128,256]{1,0:T(8,128)S(1)}, f32[128,256]{1,0:T(8,128)S(1)}, u32[]{:S(2)}, u32[]{:S(2)}) collective-permute-start(f32[128,256]{1,0:T(8,128)S(1)} %get-tuple-element.35), channel_id=1, source_target_pairs={{0,6},{1,7},{2,0},{3,1},{4,2},{5,3},{6,4},{7,5},{8,14},{9,15},{10,... | collective-permute-start | bytes 393224 | tf_op jit(solution)/shard_map/ppermute | solution.py:332
  98.8 9.4 %shard_map.22 = (f32[256,256]{1,0:T(8,128)S(1)}, f32[256,256]{1,0:T(8,128)S(1)}) custom-call(f32[256,256]{1,0:T(8,128)S(1)} %get-tuple-element.39.a, f32[256,256]{1,0:T(8,128)S(1)} %get-tuple-element.40.e_low), custom_call_target="tpu_custom_call" | custom-call | flops 1000000000 | bytes 41943040 | tf_op jit(solution)/shard_map/pallas_call | solution.py:197
  108.2 12.8 %shard_map.23 = f32[8192,128]{1,0:T(8,128)} custom-call(s32[2]{0:T(128)S(1)} %pad_add_fusion.where, f32[8192,128]{1,0:T(8,128)} %bitcast.14, f32[256,256]{1,0:T(8,128)S(1)} %get-tuple-element.30.refs_0_, f32[256,256]{1,0:T(8,128)S(1)} %collective-permute-done.3.ready1.refs_1_, f32[256,256]{1,0:T(8,128)S(1)} %collective-permute-done.4.right.refs_2_, ...), custom_call_target="tpu_custom_call" | custom-call | flops 8000000000 | bytes 12582912 | tf_op jit(solution)/shard_map/pallas_call | solution.py:309
  (15 shorter events, 0.3 us)
Async XLA Ops:
  2.9 27.9 %collective-permute-start = (f32[256,256]{1,0:T(8,128)S(1)}, f32[256,256]{1,0:T(8,128)S(1)}, u32[]{:S(2)}, u32[]{:S(2)}) collective-permute-start(f32[256,256]{1,0:T(8,128)S(1)} %get-tuple-element.25), channel_id=1, source_target_pairs={{0,7},{1,2},{8,15},{9,10},{16,23},{17,18},{24,31},{25,26},{32,39},... | collective-permute-start | bytes 786440 | tf_op jit(solution)/shard_map/ppermute | solution.py:345
  11.2 19.6 %collective-permute-start.1 = (f32[256,256]{1,0:T(8,128)S(1)}, f32[256,256]{1,0:T(8,128)S(1)}, u32[]{:S(2)}, u32[]{:S(2)}) collective-permute-start(f32[256,256]{1,0:T(8,128)S(1)} %get-tuple-element.26), channel_id=1, source_target_pairs={{0,6},{1,3},{8,14},{9,11},{16,22},{17,19},{24,30},{25,27},{32,38},... | collective-permute-start | bytes 786440 | tf_op jit(solution)/shard_map/ppermute | solution.py:345
  12.6 18.3 %collective-permute-start.2 = (f32[256,256]{1,0:T(8,128)S(1)}, f32[256,256]{1,0:T(8,128)S(1)}, u32[]{:S(2)}, u32[]{:S(2)}) collective-permute-start(f32[256,256]{1,0:T(8,128)S(1)} %get-tuple-element.27), channel_id=1, source_target_pairs={{0,5},{1,4},{8,13},{9,12},{16,21},{17,20},{24,29},{25,28},{32,37},... | collective-permute-start | bytes 786440 | tf_op jit(solution)/shard_map/ppermute | solution.py:345
  13.9 17.0 %all-to-all-start = ((f32[32,8,256]{2,1,0:T(8,128)}), f32[32,8,256]{2,1,0:T(8,128)S(1)}, u32[]{:S(2)}, u32[]{:S(2)}) async-start(f32[32,8,256]{2,1,0:T(8,128)} %bitcast.7), calls=%async_computation | async-start | bytes 524288 | tf_op jit(solution)/shard_map/all_to_all | solution.py:346
  48.3 30.5 %all-to-all-start.2 = ((f32[16,88,256]{2,1,0:T(8,128)}), f32[16,88,256]{2,1,0:T(8,128)S(1)}, u32[]{:S(2)}, u32[]{:S(2)}) async-start(f32[16,88,256]{2,1,0:T(8,128)} %get-tuple-element.31), calls=%async_computation.2 | async-start | bytes 2883584 | tf_op jit(solution)/shard_map/all_to_all | solution.py:354
  55.0 6.1 %collective-permute-start.6 = (f32[256,256]{1,0:T(8,128)S(1)}, f32[256,256]{1,0:T(8,128)S(1)}, u32[]{:S(2)}, u32[]{:S(2)}) collective-permute-start(f32[256,256]{1,0:T(8,128)S(1)} %get-tuple-element.30.refs_0_), channel_id=1, source_target_pairs={{0,7},{1,0},{2,1},{3,2},{4,3},{5,4},{6,5},{7,6},{8,15},{9,8},{10,9... | collective-permute-start | bytes 786440 | tf_op jit(solution)/shard_map/ppermute | solution.py:332
  55.1 13.9 %collective-permute-start.5 = (f32[256,256]{1,0:T(8,128)S(1)}, f32[256,256]{1,0:T(8,128)S(1)}, u32[]{:S(2)}, u32[]{:S(2)}) collective-permute-start(f32[256,256]{1,0:T(8,128)S(1)} %get-tuple-element.30.refs_0_), channel_id=1, source_target_pairs={{0,6},{1,7},{2,0},{3,1},{4,2},{5,3},{6,4},{7,5},{8,14},{9,15},{10,... | collective-permute-start | bytes 786440 | tf_op jit(solution)/shard_map/ppermute | solution.py:332
  57.4 11.7 %collective-permute-start.4 = (f32[256,256]{1,0:T(8,128)S(1)}, f32[256,256]{1,0:T(8,128)S(1)}, u32[]{:S(2)}, u32[]{:S(2)}) collective-permute-start(f32[256,256]{1,0:T(8,128)S(1)} %get-tuple-element.30.refs_0_), channel_id=1, source_target_pairs={{0,2},{1,3},{2,4},{3,5},{4,6},{5,7},{6,0},{7,1},{8,10},{9,11},{10,... | collective-permute-start | bytes 786440 | tf_op jit(solution)/shard_map/ppermute | solution.py:332
  57.6 21.2 %collective-permute-start.3 = (f32[256,256]{1,0:T(8,128)S(1)}, f32[256,256]{1,0:T(8,128)S(1)}, u32[]{:S(2)}, u32[]{:S(2)}) collective-permute-start(f32[256,256]{1,0:T(8,128)S(1)} %get-tuple-element.30.refs_0_), channel_id=1, source_target_pairs={{0,1},{1,2},{2,3},{3,4},{4,5},{5,6},{6,7},{7,0},{8,9},{9,10},{10,1... | collective-permute-start | bytes 786440 | tf_op jit(solution)/shard_map/ppermute | solution.py:332
  78.8 2.5 %collective-permute-start.11 = (f32[16,24,256]{2,1,0:T(8,128)S(1)}, f32[16,24,256]{2,1,0:T(8,128)S(1)}, u32[]{:S(2)}, u32[]{:S(2)}) collective-permute-start(f32[16,24,256]{2,1,0:T(8,128)S(1)} %get-tuple-element.36.mine), channel_id=1, source_target_pairs={{0,8},{8,0},{16,24},{24,16},{32,40},{40,32},{48,56},{56,48},{64,72... | collective-permute-start | bytes 1179656 | tf_op jit(solution)/shard_map/ppermute | solution.py:359
  92.1 16.1 %collective-permute-start.12 = (f32[16,88,256]{2,1,0:T(8,128)S(1)}, f32[16,88,256]{2,1,0:T(8,128)S(1)}, u32[]{:S(2)}, u32[]{:S(2)}) collective-permute-start(f32[16,88,256]{2,1,0:T(8,128)S(1)} %get-tuple-element.37.refs_9_), channel_id=1, source_target_pairs={{0,8},{8,0},{16,24},{24,16},{32,40},{40,32},{48,56},{56,48},{64,72... | collective-permute-start | bytes 4325384 | tf_op jit(solution)/shard_map/ppermute | solution.py:362
  92.5 15.6 %collective-permute-start.7 = (f32[256,256]{1,0:T(8,128)S(1)}, f32[256,256]{1,0:T(8,128)S(1)}, u32[]{:S(2)}, u32[]{:S(2)}) collective-permute-start(f32[256,256]{1,0:T(8,128)S(1)} %get-tuple-element.32), channel_id=1, source_target_pairs={{0,1},{1,2},{2,3},{3,4},{4,5},{5,6},{6,7},{7,0},{8,9},{9,10},{10,1... | collective-permute-start | bytes 786440 | tf_op jit(solution)/shard_map/ppermute | solution.py:332
  92.5 15.7 %collective-permute-start.8 = (f32[256,256]{1,0:T(8,128)S(1)}, f32[256,256]{1,0:T(8,128)S(1)}, u32[]{:S(2)}, u32[]{:S(2)}) collective-permute-start(f32[256,256]{1,0:T(8,128)S(1)} %get-tuple-element.33), channel_id=1, source_target_pairs={{0,7},{1,0},{2,1},{3,2},{4,3},{5,4},{6,5},{7,6},{8,15},{9,8},{10,9... | collective-permute-start | bytes 786440 | tf_op jit(solution)/shard_map/ppermute | solution.py:332
  95.2 13.0 %collective-permute-start.9 = (f32[128,256]{1,0:T(8,128)S(1)}, f32[128,256]{1,0:T(8,128)S(1)}, u32[]{:S(2)}, u32[]{:S(2)}) collective-permute-start(f32[128,256]{1,0:T(8,128)S(1)} %get-tuple-element.34), channel_id=1, source_target_pairs={{0,2},{1,3},{2,4},{3,5},{4,6},{5,7},{6,0},{7,1},{8,10},{9,11},{10,... | collective-permute-start | bytes 393224 | tf_op jit(solution)/shard_map/ppermute | solution.py:332
  95.2 13.0 %collective-permute-start.10 = (f32[128,256]{1,0:T(8,128)S(1)}, f32[128,256]{1,0:T(8,128)S(1)}, u32[]{:S(2)}, u32[]{:S(2)}) collective-permute-start(f32[128,256]{1,0:T(8,128)S(1)} %get-tuple-element.35), channel_id=1, source_target_pairs={{0,6},{1,7},{2,0},{3,1},{4,2},{5,3},{6,4},{7,5},{8,14},{9,15},{10,... | collective-permute-start | bytes 393224 | tf_op jit(solution)/shard_map/ppermute | solution.py:332

commit v6 on v5

--- a/solution.py
+++ b/solution.py
@@ -237,8 +237,8 @@
     mine, other, w00, w10, w11, out, buf, panel, mirror, x_out, left, right, x_cat, y_cat, sem_a, sem_out = refs
     r, c = where[0], where[1]
     core = lax.rem(r, 2)
-    n_half = 4 * T * 8 // 2
-    loads = [pltpu.make_async_copy(a.at[pl.ds(i * n_half, n_half)], buf.at[pl.ds(i * n_half, n_half)], sem_a.at[i]) for i in range(2)]
+    n_part = 8 * T
+    loads = [pltpu.make_async_copy(a.at[pl.ds(i * n_part, n_part)], buf.at[pl.ds(i * n_part, n_part)], sem_a.at[i]) for i in range(4)]
     for load in loads:
         load.start()
     for i, t in enumerate((w00, w10, w11)):
@@ -274,16 +274,16 @@
     first = jnp.concatenate([panel[0], panel[7], panel[6], panel[5]], axis=0)
     solve(first, panel[1:5].reshape(4 * T, T), 32, r, x_cat, (0, 1, 0), True)
 
-    rows = 2 * T
+    rows = T
     stores = []
-    for i in range(2):
+    for i in range(4):
         loads[i].wait()
         span = slice(i * rows, (i + 1) * rows)
         for n in range(4):
             cols = slice(n * T, (n + 1) * T)
             product = mul(x_cat[span], y_cat[cols])
             for half in range(2):
-                at = pl.ds(i * n_half + half * 4 + n, rows, stride=8)
+                at = pl.ds(i * n_part + half * 4 + n, rows, stride=8)
                 buf[at, :] = buf[at, :] - product[:, half * B : (half + 1) * B]
 
         @pl.when(c < 2)
@@ -294,9 +294,9 @@
             keep = (tile > c) | ((tile == c) & (lax.rem(row, T) >= col))
             x = jnp.where(keep, x_out[span], 0.0)
             for half in range(2):
-                buf[pl.ds(i * n_half + half * 4, rows, stride=8), :] = x[:, half * B : (half + 1) * B]
-
-        at = pl.ds(i * n_half, n_half)
+                buf[pl.ds(i * n_part + half * 4, rows, stride=8), :] = x[:, half * B : (half + 1) * B]
+
+        at = pl.ds(i * n_part, n_part)
         stores.append(pltpu.make_async_copy(buf.at[at], out.at[at], sem_out.at[i]))
         stores[i].start()
     for store in stores:
@@ -320,8 +320,8 @@
             pltpu.VMEM((T, 3 * SIX), BF16),
             pltpu.VMEM((4 * T, SIX), BF16),
             pltpu.VMEM((4 * T, SIX), BF16),
-            pltpu.SemaphoreType.DMA((2,)),
-            pltpu.SemaphoreType.DMA((2,)),
+            pltpu.SemaphoreType.DMA((4,)),
+            pltpu.SemaphoreType.DMA((4,)),
         ],
         compiler_params=pltpu.CompilerParams(vmem_limit_bytes=38 * MIB),
         cost_estimate=pl.CostEstimate(flops=8 * 10**9, bytes_accessed=12 * MIB, transcendentals=0),

time: 122 us -> 122 us (level)
  no operation moved by 1% of the time
where the time goes in v6:
time: 122 us; the launch traced here: 121 us
  Pallas kernels  38.2 us (31%)
  starting transfers between devices  37.5 us (31%)
  waiting for transfers between devices  30 us (25%)
  blocking collectives  15.2 us (12%)
    ppermute x8, waiting for transfers between devices, along(): return lax.ppermute(x, 'col', [(z, (z + step) % 8) for z in range(8)])  19.8 us
    all_to_all x1, blocking collectives, per_device(): lines = lax.all_to_all(spread, 'col', 0, 0)  15.2 us
    pallas_call x1, Pallas kernels, update(): pl.pallas_call(update_kernel, out_shape=jax.ShapeDtypeStruct(a.shape, F32...  12.9 us
    ppermute x3, starting transfers between devices, per_device(): lax.ppermute(column[m], 'col', [(0, 8 - m), (1, 1 + m)])  10.9 us
    pallas_call x1, Pallas kernels, first_factor(): pl.pallas_call(first_kernel, out_shape=[square(T)] * 3 + [jax.ShapeDtypeS...  10.7 us
    ppermute x8, starting transfers between devices, along(): return lax.ppermute(x, 'col', [(z, (z + step) % 8) for z in range(8)])  10.2 us
    pallas_call x1, Pallas kernels, second_factor(): pl.pallas_call(second_kernel, out_shape=[square(T)] * 2, in_specs=[VMEM]...  9.36 us
    all_to_all x1, waiting for transfers between devices, per_device(): pieces = lax.all_to_all(first.reshape(32, 8, T), 'row', 0, 0)  8.82 us
  transfers between devices with their start and end apart: 15, of which 5 were waited for; matrix products, arithmetic and copies ran while one was open for 0% of the time, Pallas kernels for 8%

profile of v6, /device:TPU:1, one launch (start us, length us, event | category | flops | bytes accessed | tf_op | source)
XLA Modules:
  0.0 121.3 jit_solution(8361919206922350871)
XLA Ops:
  0.0 2.9 %shard_map.17 = (f32[256,256]{1,0:T(8,128)}, f32[256,256]{1,0:T(8,128)S(1)}, f32[256,256]{1,0:T(8,128)S(1)}, f32[256,256]{1,0:T(8,128)S(1)}) custom-call(f32[8192,128]{1,0:T(8,128)} %bitcast.13), custom_call_target="tpu_custom_call" | custom-call | bytes 5242880 | tf_op jit(solution)/shard_map/pallas_call | solution.py:105
  2.9 8.3 %collective-permute-start = (f32[256,256]{1,0:T(8,128)S(1)}, f32[256,256]{1,0:T(8,128)S(1)}, u32[]{:S(2)}, u32[]{:S(2)}) collective-permute-start(f32[256,256]{1,0:T(8,128)S(1)} %get-tuple-element.25), channel_id=1, source_target_pairs={{0,7},{1,2},{8,15},{9,10},{16,23},{17,18},{24,31},{25,26},{32,39},... | collective-permute-start | bytes 786440 | tf_op jit(solution)/shard_map/ppermute | solution.py:345
  11.2 1.3 %collective-permute-start.1 = (f32[256,256]{1,0:T(8,128)S(1)}, f32[256,256]{1,0:T(8,128)S(1)}, u32[]{:S(2)}, u32[]{:S(2)}) collective-permute-start(f32[256,256]{1,0:T(8,128)S(1)} %get-tuple-element.26), channel_id=1, source_target_pairs={{0,6},{1,3},{8,14},{9,11},{16,22},{17,19},{24,30},{25,27},{32,38},... | collective-permute-start | bytes 786440 | tf_op jit(solution)/shard_map/ppermute | solution.py:345
  12.6 1.3 %collective-permute-start.2 = (f32[256,256]{1,0:T(8,128)S(1)}, f32[256,256]{1,0:T(8,128)S(1)}, u32[]{:S(2)}, u32[]{:S(2)}) collective-permute-start(f32[256,256]{1,0:T(8,128)S(1)} %get-tuple-element.27), channel_id=1, source_target_pairs={{0,5},{1,4},{8,13},{9,12},{16,21},{17,20},{24,29},{25,28},{32,37},... | collective-permute-start | bytes 786440 | tf_op jit(solution)/shard_map/ppermute | solution.py:345
  13.9 8.1 %all-to-all-start = ((f32[32,8,256]{2,1,0:T(8,128)}), f32[32,8,256]{2,1,0:T(8,128)S(1)}, u32[]{:S(2)}, u32[]{:S(2)}) async-start(f32[32,8,256]{2,1,0:T(8,128)} %bitcast.7), calls=%async_computation | async-start | bytes 524288 | tf_op jit(solution)/shard_map/all_to_all | solution.py:346
  22.0 8.8 %all-to-all-done.pieces = f32[32,8,256]{2,1,0:T(8,128)S(1)} async-done(((f32[32,8,256]{2,1,0:T(8,128)}), f32[32,8,256]{2,1,0:T(8,128)S(1)}, u32[]{:S(2)}, u32[]{:S(2)}) %all-to-all-start) | async-done | bytes 262176 | tf_op jit(solution)/shard_map/all_to_all | solution.py:346
  30.8 1.0 shard_map.18
  31.9 15.2 %all_to_all.15.lines = f32[8,48,256]{2,1,0:T(8,128)S(1)} all-to-all(f32[8,48,256]{2,1,0:T(8,128)S(1)} %get-tuple-element.28), channel_id=1, replica_groups=mesh['row'=32,'col'=8] {'col'}, dimensions={0} | all-to-all | bytes 786432 | tf_op jit(solution)/shard_map/all_to_all | solution.py:348
  47.1 1.2 shard_map.19
  48.3 6.8 %all-to-all-start.2 = ((f32[16,88,256]{2,1,0:T(8,128)}), f32[16,88,256]{2,1,0:T(8,128)S(1)}, u32[]{:S(2)}, u32[]{:S(2)}) async-start(f32[16,88,256]{2,1,0:T(8,128)} %get-tuple-element.31), calls=%async_computation.2 | async-start | bytes 2883584 | tf_op jit(solution)/shard_map/all_to_all | solution.py:354
  55.1 2.3 %collective-permute-start.5 = (f32[256,256]{1,0:T(8,128)S(1)}, f32[256,256]{1,0:T(8,128)S(1)}, u32[]{:S(2)}, u32[]{:S(2)}) collective-permute-start(f32[256,256]{1,0:T(8,128)S(1)} %get-tuple-element.30.refs_0_), channel_id=1, source_target_pairs={{0,6},{1,7},{2,0},{3,1},{4,2},{5,3},{6,4},{7,5},{8,14},{9,15},{10,... | collective-permute-start | bytes 786440 | tf_op jit(solution)/shard_map/ppermute | solution.py:332
  57.4 0.2 collective-permute-start.4
  57.6 1.4 %collective-permute-start.3 = (f32[256,256]{1,0:T(8,128)S(1)}, f32[256,256]{1,0:T(8,128)S(1)}, u32[]{:S(2)}, u32[]{:S(2)}) collective-permute-start(f32[256,256]{1,0:T(8,128)S(1)} %get-tuple-element.30.refs_0_), channel_id=1, source_target_pairs={{0,1},{1,2},{2,3},{3,4},{4,5},{5,6},{6,7},{7,0},{8,9},{9,10},{10,1... | collective-permute-start | bytes 786440 | tf_op jit(solution)/shard_map/ppermute | solution.py:332
  59.0 2.2 %collective-permute-done.6.ready2.refs_6_ = f32[256,256]{1,0:T(8,128)S(1)} collective-permute-done((f32[256,256]{1,0:T(8,128)S(1)}, f32[256,256]{1,0:T(8,128)S(1)}, u32[]{:S(2)}, u32[]{:S(2)}) %collective-permute-start.6) | collective-permute-done | bytes 262176 | tf_op jit(solution)/shard_map/ppermute | solution.py:332
  61.1 7.9 %collective-permute-done.5.left.refs_5_ = f32[256,256]{1,0:T(8,128)S(1)} collective-permute-done((f32[256,256]{1,0:T(8,128)S(1)}, f32[256,256]{1,0:T(8,128)S(1)}, u32[]{:S(2)}, u32[]{:S(2)}) %collective-permute-start.5) | collective-permute-done | bytes 262176 | tf_op jit(solution)/shard_map/ppermute | solution.py:332
  69.1 9.7 %collective-permute-done.3.ready1.refs_1_ = f32[256,256]{1,0:T(8,128)S(1)} collective-permute-done((f32[256,256]{1,0:T(8,128)S(1)}, f32[256,256]{1,0:T(8,128)S(1)}, u32[]{:S(2)}, u32[]{:S(2)}) %collective-permute-start.3) | collective-permute-done | bytes 262176 | tf_op jit(solution)/shard_map/ppermute | solution.py:332
  78.8 1.2 collective-permute-start.11
  80.0 1.3 %collective-permute-done.11.other = f32[16,24,256]{2,1,0:T(8,128)S(1)} collective-permute-done((f32[16,24,256]{2,1,0:T(8,128)S(1)}, f32[16,24,256]{2,1,0:T(8,128)S(1)}, u32[]{:S(2)}, u32[]{:S(2)}) %collective-permute-start.11) | collective-permute-done | bytes 393248 | tf_op jit(solution)/shard_map/ppermute | solution.py:359
  81.4 10.7 %shard_map.21 = (f32[256,256]{1,0:T(8,128)S(1)}, f32[256,256]{1,0:T(8,128)S(1)}, f32[256,256]{1,0:T(8,128)S(1)}, f32[16,88,256]{2,1,0:T(8,128)S(1)}) custom-call(s32[2]{0:T(128)S(1)} %pad_add_fusion.where, f32[16,24,256]{2,1,0:T(8,128)S(1)} %get-tuple-element.36.mine, ...), custom_call_target="tpu_custom_call", output_to_operand_aliasing={{3}: (3, {})} | custom-call | flops 1000000000 | bytes 41943040 | tf_op jit(solution)/shard_map/pallas_call | solution.py:184
  92.1 0.5 collective-permute-start.12
  92.5 2.7 %collective-permute-start.8 = (f32[256,256]{1,0:T(8,128)S(1)}, f32[256,256]{1,0:T(8,128)S(1)}, u32[]{:S(2)}, u32[]{:S(2)}) collective-permute-start(f32[256,256]{1,0:T(8,128)S(1)} %get-tuple-element.33), channel_id=1, source_target_pairs={{0,7},{1,0},{2,1},{3,2},{4,3},{5,4},{6,5},{7,6},{8,15},{9,8},{10,9... | collective-permute-start | bytes 786440 | tf_op jit(solution)/shard_map/ppermute | solution.py:332
  95.2 3.6 %collective-permute-start.10 = (f32[128,256]{1,0:T(8,128)S(1)}, f32[128,256]{1,0:T(8,128)S(1)}, u32[]{:S(2)}, u32[]{:S(2)}) collective-permute-start(f32[128,256]{1,0:T(8,128)S(1)} %get-tuple-element.35), channel_id=1, source_target_pairs={{0,6},{1,7},{2,0},{3,1},{4,2},{5,3},{6,4},{7,5},{8,14},{9,15},{10,... | collective-permute-start | bytes 393224 | tf_op jit(solution)/shard_map/ppermute | solution.py:332
  98.8 9.4 %shard_map.22 = (f32[256,256]{1,0:T(8,128)S(1)}, f32[256,256]{1,0:T(8,128)S(1)}) custom-call(f32[256,256]{1,0:T(8,128)S(1)} %get-tuple-element.39.a, f32[256,256]{1,0:T(8,128)S(1)} %get-tuple-element.40.e_low), custom_call_target="tpu_custom_call" | custom-call | flops 1000000000 | bytes 41943040 | tf_op jit(solution)/shard_map/pallas_call | solution.py:197
  108.2 12.9 %shard_map.23 = f32[8192,128]{1,0:T(8,128)} custom-call(s32[2]{0:T(128)S(1)} %pad_add_fusion.where, f32[8192,128]{1,0:T(8,128)} %bitcast.14, f32[256,256]{1,0:T(8,128)S(1)} %get-tuple-element.30.refs_0_, f32[256,256]{1,0:T(8,128)S(1)} %collective-permute-done.3.ready1.refs_1_, f32[256,256]{1,0:T(8,128)S(1)} %collective-permute-done.4.right.refs_2_, ...), custom_call_target="tpu_custom_call" | custom-call | flops 8000000000 | bytes 12582912 | tf_op jit(solution)/shard_map/pallas_call | solution.py:309
  (15 shorter events, 0.3 us)
Async XLA Ops:
  2.9 27.9 %collective-permute-start = (f32[256,256]{1,0:T(8,128)S(1)}, f32[256,256]{1,0:T(8,128)S(1)}, u32[]{:S(2)}, u32[]{:S(2)}) collective-permute-start(f32[256,256]{1,0:T(8,128)S(1)} %get-tuple-element.25), channel_id=1, source_target_pairs={{0,7},{1,2},{8,15},{9,10},{16,23},{17,18},{24,31},{25,26},{32,39},... | collective-permute-start | bytes 786440 | tf_op jit(solution)/shard_map/ppermute | solution.py:345
  11.2 19.6 %collective-permute-start.1 = (f32[256,256]{1,0:T(8,128)S(1)}, f32[256,256]{1,0:T(8,128)S(1)}, u32[]{:S(2)}, u32[]{:S(2)}) collective-permute-start(f32[256,256]{1,0:T(8,128)S(1)} %get-tuple-element.26), channel_id=1, source_target_pairs={{0,6},{1,3},{8,14},{9,11},{16,22},{17,19},{24,30},{25,27},{32,38},... | collective-permute-start | bytes 786440 | tf_op jit(solution)/shard_map/ppermute | solution.py:345
  12.6 18.3 %collective-permute-start.2 = (f32[256,256]{1,0:T(8,128)S(1)}, f32[256,256]{1,0:T(8,128)S(1)}, u32[]{:S(2)}, u32[]{:S(2)}) collective-permute-start(f32[256,256]{1,0:T(8,128)S(1)} %get-tuple-element.27), channel_id=1, source_target_pairs={{0,5},{1,4},{8,13},{9,12},{16,21},{17,20},{24,29},{25,28},{32,37},... | collective-permute-start | bytes 786440 | tf_op jit(solution)/shard_map/ppermute | solution.py:345
  13.9 17.0 %all-to-all-start = ((f32[32,8,256]{2,1,0:T(8,128)}), f32[32,8,256]{2,1,0:T(8,128)S(1)}, u32[]{:S(2)}, u32[]{:S(2)}) async-start(f32[32,8,256]{2,1,0:T(8,128)} %bitcast.7), calls=%async_computation | async-start | bytes 524288 | tf_op jit(solution)/shard_map/all_to_all | solution.py:346
  48.3 30.5 %all-to-all-start.2 = ((f32[16,88,256]{2,1,0:T(8,128)}), f32[16,88,256]{2,1,0:T(8,128)S(1)}, u32[]{:S(2)}, u32[]{:S(2)}) async-start(f32[16,88,256]{2,1,0:T(8,128)} %get-tuple-element.31), calls=%async_computation.2 | async-start | bytes 2883584 | tf_op jit(solution)/shard_map/all_to_all | solution.py:354
  55.0 6.1 %collective-permute-start.6 = (f32[256,256]{1,0:T(8,128)S(1)}, f32[256,256]{1,0:T(8,128)S(1)}, u32[]{:S(2)}, u32[]{:S(2)}) collective-permute-start(f32[256,256]{1,0:T(8,128)S(1)} %get-tuple-element.30.refs_0_), channel_id=1, source_target_pairs={{0,7},{1,0},{2,1},{3,2},{4,3},{5,4},{6,5},{7,6},{8,15},{9,8},{10,9... | collective-permute-start | bytes 786440 | tf_op jit(solution)/shard_map/ppermute | solution.py:332
  55.1 13.9 %collective-permute-start.5 = (f32[256,256]{1,0:T(8,128)S(1)}, f32[256,256]{1,0:T(8,128)S(1)}, u32[]{:S(2)}, u32[]{:S(2)}) collective-permute-start(f32[256,256]{1,0:T(8,128)S(1)} %get-tuple-element.30.refs_0_), channel_id=1, source_target_pairs={{0,6},{1,7},{2,0},{3,1},{4,2},{5,3},{6,4},{7,5},{8,14},{9,15},{10,... | collective-permute-start | bytes 786440 | tf_op jit(solution)/shard_map/ppermute | solution.py:332
  57.4 11.7 %collective-permute-start.4 = (f32[256,256]{1,0:T(8,128)S(1)}, f32[256,256]{1,0:T(8,128)S(1)}, u32[]{:S(2)}, u32[]{:S(2)}) collective-permute-start(f32[256,256]{1,0:T(8,128)S(1)} %get-tuple-element.30.refs_0_), channel_id=1, source_target_pairs={{0,2},{1,3},{2,4},{3,5},{4,6},{5,7},{6,0},{7,1},{8,10},{9,11},{10,... | collective-permute-start | bytes 786440 | tf_op jit(solution)/shard_map/ppermute | solution.py:332
  57.6 21.2 %collective-permute-start.3 = (f32[256,256]{1,0:T(8,128)S(1)}, f32[256,256]{1,0:T(8,128)S(1)}, u32[]{:S(2)}, u32[]{:S(2)}) collective-permute-start(f32[256,256]{1,0:T(8,128)S(1)} %get-tuple-element.30.refs_0_), channel_id=1, source_target_pairs={{0,1},{1,2},{2,3},{3,4},{4,5},{5,6},{6,7},{7,0},{8,9},{9,10},{10,1... | collective-permute-start | bytes 786440 | tf_op jit(solution)/shard_map/ppermute | solution.py:332
  78.8 2.5 %collective-permute-start.11 = (f32[16,24,256]{2,1,0:T(8,128)S(1)}, f32[16,24,256]{2,1,0:T(8,128)S(1)}, u32[]{:S(2)}, u32[]{:S(2)}) collective-permute-start(f32[16,24,256]{2,1,0:T(8,128)S(1)} %get-tuple-element.36.mine), channel_id=1, source_target_pairs={{0,8},{8,0},{16,24},{24,16},{32,40},{40,32},{48,56},{56,48},{64,72... | collective-permute-start | bytes 1179656 | tf_op jit(solution)/shard_map/ppermute | solution.py:359
  92.1 16.1 %collective-permute-start.12 = (f32[16,88,256]{2,1,0:T(8,128)S(1)}, f32[16,88,256]{2,1,0:T(8,128)S(1)}, u32[]{:S(2)}, u32[]{:S(2)}) collective-permute-start(f32[16,88,256]{2,1,0:T(8,128)S(1)} %get-tuple-element.37.refs_9_), channel_id=1, source_target_pairs={{0,8},{8,0},{16,24},{24,16},{32,40},{40,32},{48,56},{56,48},{64,72... | collective-permute-start | bytes 4325384 | tf_op jit(solution)/shard_map/ppermute | solution.py:362
  92.5 15.6 %collective-permute-start.7 = (f32[256,256]{1,0:T(8,128)S(1)}, f32[256,256]{1,0:T(8,128)S(1)}, u32[]{:S(2)}, u32[]{:S(2)}) collective-permute-start(f32[256,256]{1,0:T(8,128)S(1)} %get-tuple-element.32), channel_id=1, source_target_pairs={{0,1},{1,2},{2,3},{3,4},{4,5},{5,6},{6,7},{7,0},{8,9},{9,10},{10,1... | collective-permute-start | bytes 786440 | tf_op jit(solution)/shard_map/ppermute | solution.py:332
  92.5 15.7 %collective-permute-start.8 = (f32[256,256]{1,0:T(8,128)S(1)}, f32[256,256]{1,0:T(8,128)S(1)}, u32[]{:S(2)}, u32[]{:S(2)}) collective-permute-start(f32[256,256]{1,0:T(8,128)S(1)} %get-tuple-element.33), channel_id=1, source_target_pairs={{0,7},{1,0},{2,1},{3,2},{4,3},{5,4},{6,5},{7,6},{8,15},{9,8},{10,9... | collective-permute-start | bytes 786440 | tf_op jit(solution)/shard_map/ppermute | solution.py:332
  95.2 13.0 %collective-permute-start.9 = (f32[128,256]{1,0:T(8,128)S(1)}, f32[128,256]{1,0:T(8,128)S(1)}, u32[]{:S(2)}, u32[]{:S(2)}) collective-permute-start(f32[128,256]{1,0:T(8,128)S(1)} %get-tuple-element.34), channel_id=1, source_target_pairs={{0,2},{1,3},{2,4},{3,5},{4,6},{5,7},{6,0},{7,1},{8,10},{9,11},{10,... | collective-permute-start | bytes 393224 | tf_op jit(solution)/shard_map/ppermute | solution.py:332
  95.2 13.0 %collective-permute-start.10 = (f32[128,256]{1,0:T(8,128)S(1)}, f32[128,256]{1,0:T(8,128)S(1)}, u32[]{:S(2)}, u32[]{:S(2)}) collective-permute-start(f32[128,256]{1,0:T(8,128)S(1)} %get-tuple-element.35), channel_id=1, source_target_pairs={{0,6},{1,7},{2,0},{3,1},{4,2},{5,3},{6,4},{7,5},{8,14},{9,15},{10,... | collective-permute-start | bytes 393224 | tf_op jit(solution)/shard_map/ppermute | solution.py:332
